TPU v7x, 128 devices: a whole 4x4x4 slice. The times are simulated.
128 devices in a mesh: scene: 32 (over x, y, core), grp: 4 (over z).
Axes of the slice: x: 4, y: 4, z: 4, core: 2. Of those that a mesh axis runs over, the one named last changes fastest.
Arguments:
- windows: bfloat16 [128, 4, 512, 512], P(('scene', 'grp')), may hold values from -6 to 6
- counts: int32 [128], P(('scene', 'grp')), may hold values from 1 to 4, as said below
- intersection_pairs: int32 [128, 4], P(('scene', 'grp')), may hold values from 0 to 127, as said below
Outputs:
- surfaces: float32 [128, 4, 512, 512], P(('scene', 'grp'))
Inputs may be any that keep to these rules, and one draw needn't show every extreme that they name: The counts of all scenes sum to 256. `intersection_pairs`: columns are scene, window, scene, window. Every slot (s, w) with w < counts[s] is named exactly once in the whole list; no other slot is named.
All inputs are finite; a program needn't handle non-finite values.
Results may differ from a plain program's by a relative error of at most 0.009.
Values may be sent and summed in bfloat16 or wider, within the bound.
No kernel may reach another device: no remote copies, remote signals or barrier semaphores. Data moves between devices by JAX's collectives and lax.ppermute only.
A program may use at most 128 MiB of HBM per device.

v0:
```python
import functools

import jax
import jax.numpy as jnp
import numpy as np
from jax import lax
from jax.experimental import pallas as pl
from jax.experimental.pallas import tpu as pltpu
from jax.sharding import PartitionSpec as P

AXES = ("scene", "grp")
LENGTH = 512
SLOTS_HELD = 4
LANES = 128
LANE_BLOCKS = LENGTH // LANES
BF16 = jnp.bfloat16
F32 = jnp.float32


def packed_tables(devices):
    places = np.arange(LENGTH)
    packed = LENGTH // devices
    forward = np.zeros((devices, packed, LENGTH))
    backward = np.zeros((devices, packed, LENGTH))
    for dev in range(devices):
        for part in range(packed):
            freq = dev * (packed // 2) + part // 2
            angle = 2.0 * np.pi * ((freq * places) % LENGTH) / LENGTH
            if part % 2 == 0:
                forward[dev, part] = np.cos(angle)
                backward[dev, part] = np.cos(angle) * (1.0 if freq == 0 else 2.0)
            elif freq == 0:
                forward[dev, part] = 1.0 - 2.0 * (places % 2)
                backward[dev, part] = 1.0 - 2.0 * (places % 2)
            else:
                forward[dev, part] = -np.sin(angle)
                backward[dev, part] = -2.0 * np.sin(angle)
    forward = forward.reshape(2, devices // 2, packed, LENGTH).transpose(1, 0, 2, 3)
    forward = forward.reshape(LENGTH, LENGTH).astype(jnp.bfloat16)
    backward = backward.reshape(LENGTH, LENGTH).T / LENGTH
    product = places[:, None] * places[None, :] % LENGTH
    angle = 2.0 * np.pi * product / LENGTH
    both = np.concatenate([np.cos(angle), np.sin(angle)], axis=1)
    row_sum = forward.astype(np.float64).sum(axis=1)
    row_sum = np.broadcast_to(row_sum[:, None], (LENGTH, LANES)).astype(np.float32)
    return forward, row_sum, both.astype(jnp.bfloat16), backward.astype(jnp.bfloat16)


def split_rows(value, rows):
    return value.reshape(value.shape[0] // rows, rows, value.shape[1])


def forward_kernel(pair_ref, x_ref, table_ref, sum_ref, out_ref):
    half = pl.program_id(0)
    groups = LENGTH // 8
    entries = float(LENGTH * LENGTH)
    spectra = []
    for j in range(2):
        values = x_ref[j].astype(F32)
        mean = jnp.sum(values) / entries
        centered = values - mean
        scale = lax.rsqrt(jnp.sum(centered * centered) / entries + 1e-05)
        product = jnp.dot(table_ref[...], x_ref[j], preferred_element_type=F32)
        shift = jnp.concatenate([sum_ref[...] * mean] * LANE_BLOCKS, axis=1)
        spectra.append(split_rows((product - shift) * scale, 8))
    first, second = spectra
    upper = lax.broadcasted_iota(jnp.int32, first.shape, 1) < 4
    low = jnp.where(upper, first, pltpu.roll(second, 4, 1)).astype(BF16)
    high = jnp.where(upper, pltpu.roll(first, 4, 1), second).astype(BF16)
    for step in range(2):
        @pl.when(half == step)
        def _():
            for block in range(LANE_BLOCKS):
                rows = pl.ds(block * 16 + step * 8, 8)
                lanes = slice(block * LANES, (block + 1) * LANES)
                out_ref[pl.ds(0, groups), rows, :] = low[:, :, lanes]
                out_ref[pl.ds(groups, groups), rows, :] = high[:, :, lanes]
    row = lax.broadcasted_iota(jnp.int32, (8, LANES), 0)
    named = jnp.zeros((8, LANES), F32)
    for column in range(4):
        named = jnp.where(row == column, pair_ref[0, column].astype(F32), named)
    out_ref[:, pl.ds(LANE_BLOCKS * 16, 8), :] = jnp.broadcast_to(
        named[None], (2 * groups, 8, LANES)
    ).astype(BF16)


def cross_kernel(first_ref, m_ref, both_ref, out_ref, rows_ref, names_ref):
    devices = m_ref.shape[0]
    slots = devices * SLOTS_HELD
    pairs = devices
    is_first = first_ref[0] == 0
    table = both_ref[...]

    names_ref[...] = m_ref[:, pl.ds(LANE_BLOCKS * 16, 8), :].astype(F32).reshape(devices * 8, LANES)
    named = [names_ref[pl.ds(column, devices, stride=8), :] for column in range(4)]
    slot_rows = [
        (named[2 * side] * SLOTS_HELD + named[2 * side + 1]).astype(jnp.int32) for side in range(2)
    ]
    same = lax.broadcasted_iota(jnp.int32, (pairs, LANES), 0) == lax.broadcasted_iota(
        jnp.int32, (pairs, LANES), 1
    )
    slot_lanes = [
        jnp.sum(jnp.where(same, slot_rows[side], 0), axis=0, keepdims=True) for side in range(2)
    ]
    wanted = jnp.concatenate(
        [jnp.concatenate([slot_rows[side]] * (slots // LANES), axis=1) for side in range(2)], axis=0
    )
    pick = (wanted == lax.broadcasted_iota(jnp.int32, (2 * pairs, slots), 1)).astype(F32).astype(BF16)

    for block in range(LANE_BLOCKS):
        rows_ref[block] = m_ref[:, pl.ds(block * 16, 16), :].astype(F32).reshape(devices * 16, LANES)

    def part_rows(part):
        return jnp.concatenate(
            [rows_ref[block, pl.ds(part, slots, stride=4), :] for block in range(LANE_BLOCKS)], axis=1
        ).astype(BF16)

    inverse = []
    for freq in range(2):
        products = []
        for part in (2 * freq, 2 * freq + 1):
            picked = jnp.dot(pick, part_rows(part), preferred_element_type=F32).astype(BF16)
            products.append(jnp.dot(picked, table, preferred_element_type=F32))
        re_cos, re_sin = products[0][:, :LENGTH], products[0][:, LENGTH:]
        im_cos, im_sin = products[1][:, :LENGTH], products[1][:, LENGTH:]

        def cross(real, imag):
            own_real, other_real = real[:pairs], real[pairs:]
            own_imag, other_imag = imag[:pairs], imag[pairs:]
            return (
                own_real * other_real + own_imag * other_imag,
                own_imag * other_real - own_real * other_imag,
            )

        cross_real, cross_imag = cross(re_cos + im_sin, im_cos - re_sin)
        if freq == 0:
            low_real, low_imag = cross(re_cos, -re_sin)
            top_real, top_imag = cross(im_cos, -im_sin)
            cross_real = jnp.where(is_first, low_real - top_imag, cross_real)
            cross_imag = jnp.where(is_first, low_imag + top_real, cross_imag)
        crossed = jnp.concatenate([cross_real, cross_imag], axis=0).astype(BF16)
        back = jnp.dot(crossed, table, preferred_element_type=F32) * (1.0 / (LENGTH * LENGTH))
        real_cos, real_sin = back[:pairs, :LENGTH], back[:pairs, LENGTH:]
        imag_cos, imag_sin = back[pairs:, :LENGTH], back[pairs:, LENGTH:]
        own_imag = imag_cos + real_sin
        other_imag = real_sin - imag_cos
        if freq == 0:
            other_imag = jnp.where(is_first, imag_cos - real_sin, other_imag)
        inverse.append(
            jnp.concatenate(
                [real_cos - imag_sin, real_cos + imag_sin, own_imag, other_imag], axis=0
            ).astype(BF16)
        )

    row = lax.broadcasted_iota(jnp.int32, (devices * 8, 4 * pairs), 0)
    row_code = row // 8 * SLOTS_HELD + row % SLOTS_HELD + row // SLOTS_HELD % 2 * slots
    lane_code = jnp.concatenate(
        [slot_lanes[0], slot_lanes[1], slot_lanes[0] + slots, slot_lanes[1] + slots], axis=1
    )
    place = (row_code == lane_code).astype(F32).astype(BF16)
    placed = [
        split_rows(jnp.dot(place, inverse[freq], preferred_element_type=F32), 8)
        for freq in range(2)
    ]
    placed = jnp.concatenate(placed, axis=1).astype(BF16)
    for block in range(LANE_BLOCKS):
        out_ref[:, pl.ds(block * 16, 16), :] = placed[:, :, block * LANES : (block + 1) * LANES]


def surface_kernel(count_ref, m_ref, table_ref, out_ref, rows_ref):
    devices = m_ref.shape[0]
    slot = pl.program_id(0)

    @pl.when(slot == 0)
    def _():
        for block in range(LANE_BLOCKS):
            rows_ref[block] = (
                m_ref[:, pl.ds(block * 16, 16), :].astype(F32).reshape(devices * 16, LANES)
            )

    for step in range(SLOTS_HELD):
        @pl.when(slot == step)
        def _():
            rows = jnp.concatenate(
                [
                    rows_ref[block, pl.ds(step, LENGTH, stride=SLOTS_HELD), :]
                    for block in range(LANE_BLOCKS)
                ],
                axis=1,
            ).astype(BF16)
            keep = (step < count_ref[0]).astype(F32)
            out_ref[0, 0] = jnp.dot(table_ref[...], rows, preferred_element_type=F32) * keep


def per_device(windows, counts, intersection_pairs):
    devices = lax.axis_size(AXES)
    position = lax.axis_index(AXES).astype(jnp.int32).reshape(1)
    forward, row_sum, both, backward = packed_tables(devices)
    smem = pl.BlockSpec(memory_space=pltpu.SMEM)
    whole = lambda *shape: pl.BlockSpec(shape, lambda *_: (0,) * len(shape))
    params = lambda: pltpu.CompilerParams(vmem_limit_bytes=56 << 20)
    chunk_rows = LANE_BLOCKS * 16

    sent = pl.pallas_call(
        forward_kernel,
        grid=(2,),
        in_specs=[
            smem,
            pl.BlockSpec((2, LENGTH, LENGTH), lambda h: (h, 0, 0)),
            whole(LENGTH, LENGTH),
            whole(LENGTH, LANES),
        ],
        out_specs=whole(devices, chunk_rows + 8, LANES),
        out_shape=jax.ShapeDtypeStruct((devices, chunk_rows + 8, LANES), BF16),
        compiler_params=params(),
        name="forward_rows",
    )(intersection_pairs, windows[0], jnp.asarray(forward), jnp.asarray(row_sum))
    moved = lax.all_to_all(sent, AXES, 0, 0, tiled=True)
    crossed = pl.pallas_call(
        cross_kernel,
        grid=(1,),
        in_specs=[
            smem,
            whole(devices, chunk_rows + 8, LANES),
            whole(LENGTH, 2 * LENGTH),
        ],
        out_specs=whole(devices, chunk_rows, LANES),
        out_shape=jax.ShapeDtypeStruct((devices, chunk_rows, LANES), BF16),
        scratch_shapes=[
            pltpu.VMEM((LANE_BLOCKS, devices * 16, LANES), F32),
            pltpu.VMEM((devices * 8, LANES), F32),
        ],
        compiler_params=params(),
        name="cross_columns",
    )(position, moved, jnp.asarray(both))
    returned = lax.all_to_all(crossed, AXES, 0, 0, tiled=True)
    return pl.pallas_call(
        surface_kernel,
        grid=(SLOTS_HELD,),
        in_specs=[
            smem,
            whole(devices, chunk_rows, LANES),
            whole(LENGTH, LENGTH),
        ],
        out_specs=pl.BlockSpec((1, 1, LENGTH, LENGTH), lambda s: (0, s, 0, 0)),
        out_shape=jax.ShapeDtypeStruct((1, SLOTS_HELD, LENGTH, LENGTH), F32),
        scratch_shapes=[pltpu.VMEM((LANE_BLOCKS, devices * 16, LANES), F32)],
        compiler_params=params(),
        name="surfaces",
    )(counts, returned, jnp.asarray(backward))


def solution(mesh):
    in_specs = (P(AXES, None, None, None), P(AXES), P(AXES, None))
    out_specs = P(AXES, None, None, None)
    return jax.shard_map(
        per_device, mesh=mesh, in_specs=in_specs, out_specs=out_specs, check_vma=False
    )
```

profile of v0, /device:TPU:1, one launch (start us, length us, event | category | flops | bytes accessed | tf_op | source)
XLA Modules:
  0.0 103.2 jit_solution(16208044161858450569)
XLA Ops:
  0.0 7.1 %forward_rows.1 = bf16[128,72,128]{2,1,0:T(8,128)(2,1)} custom-call(s32[1,4]{1,0:T(1,128)} %pair_ref.1, bf16[4,512,512]{2,1,0:T(8,128)(2,1)} %bitcast.2, bf16[512,512]{1,0:T(8,128)(2,1)} %constant.19.clone.table_ref, f32[512,128]{1,0:T(8,128)} %constant.20.clone.sum_ref), custom_call_target="tpu_custom_call" | custom-call | tf_op jit(solution)/shard_map/forward_rows/pallas_call | solution.py:204
  7.1 11.5 %all-to-all-start = ((bf16[128,72,128]{2,1,0:T(8,128)(2,1)}), bf16[128,72,128]{2,1,0:T(8,128)(2,1)S(1)}, u32[]{:S(2)}, u32[]{:S(2)}) async-start(bf16[128,72,128]{2,1,0:T(8,128)(2,1)} %forward_rows.1), calls=%async_computation | async-start | bytes 4718592 | tf_op jit(solution)/shard_map/all_to_all | solution.py:218
  18.6 33.6 %all-to-all-done.m_ref = bf16[128,72,128]{2,1,0:T(8,128)(2,1)S(1)} async-done(((bf16[128,72,128]{2,1,0:T(8,128)(2,1)}), bf16[128,72,128]{2,1,0:T(8,128)(2,1)S(1)}, u32[]{:S(2)}, u32[]{:S(2)}) %all-to-all-start) | async-done | bytes 2359328 | tf_op jit(solution)/shard_map/all_to_all | solution.py:218
  52.3 0.0 copy-start
  52.3 1.4 %copy-done = bf16[128,72,128]{2,1,0:T(8,128)(2,1)} copy-done((bf16[128,72,128]{2,1,0:T(8,128)(2,1)}, bf16[128,72,128]{2,1,0:T(8,128)(2,1)S(1)}, u32[]{:S(2)}) %copy-start) | copy-done | bytes 2359320
  53.7 8.0 %cross_columns.1 = bf16[128,64,128]{2,1,0:T(8,128)(2,1)} custom-call(s32[1]{0:T(128)} %bitcast.first_ref, bf16[128,72,128]{2,1,0:T(8,128)(2,1)} %copy-done, bf16[512,1024]{1,0:T(8,128)(2,1)} %constant.21.clone.both_ref), custom_call_target="tpu_custom_call" | custom-call | tf_op jit(solution)/shard_map/cross_columns/pallas_call | solution.py:219
  61.7 3.8 %all-to-all-start.1 = ((bf16[128,64,128]{2,1,0:T(8,128)(2,1)}), bf16[128,64,128]{2,1,0:T(8,128)(2,1)S(1)}, u32[]{:S(2)}, u32[]{:S(2)}) async-start(bf16[128,64,128]{2,1,0:T(8,128)(2,1)} %cross_columns.1), calls=%async_computation.1 | async-start | bytes 4194304 | tf_op jit(solution)/shard_map/all_to_all | solution.py:236
  66.2 30.3 %all-to-all-done.1.m_ref = bf16[128,64,128]{2,1,0:T(8,128)(2,1)S(1)} async-done(((bf16[128,64,128]{2,1,0:T(8,128)(2,1)}), bf16[128,64,128]{2,1,0:T(8,128)(2,1)S(1)}, u32[]{:S(2)}, u32[]{:S(2)}) %all-to-all-start.1) | async-done | bytes 2097184 | tf_op jit(solution)/shard_map/all_to_all | solution.py:236
  96.5 0.0 copy-start.1
  96.5 1.3 %copy-done.1 = bf16[128,64,128]{2,1,0:T(8,128)(2,1)} copy-done((bf16[128,64,128]{2,1,0:T(8,128)(2,1)}, bf16[128,64,128]{2,1,0:T(8,128)(2,1)S(1)}, u32[]{:S(2)}) %copy-start.1) | copy-done | bytes 2097176
  97.8 5.3 %surfaces.1 = f32[1,4,512,512]{3,2,1,0:T(8,128)} custom-call(s32[1]{0:T(128)S(6)} %copy.8.count_ref, bf16[128,64,128]{2,1,0:T(8,128)(2,1)} %copy-done.1, bf16[512,512]{1,0:T(8,128)(2,1)} %constant.22.clone.table_ref), custom_call_target="tpu_custom_call" | custom-call | tf_op jit(solution)/shard_map/surfaces/pallas_call | solution.py:237
Async XLA Ops:
  7.1 45.1 %all-to-all-start = ((bf16[128,72,128]{2,1,0:T(8,128)(2,1)}), bf16[128,72,128]{2,1,0:T(8,128)(2,1)S(1)}, u32[]{:S(2)}, u32[]{:S(2)}) async-start(bf16[128,72,128]{2,1,0:T(8,128)(2,1)} %forward_rows.1), calls=%async_computation | async-start | bytes 4718592 | tf_op jit(solution)/shard_map/all_to_all | solution.py:218
  52.3 1.4 %copy-start = (bf16[128,72,128]{2,1,0:T(8,128)(2,1)}, bf16[128,72,128]{2,1,0:T(8,128)(2,1)S(1)}, u32[]{:S(2)}) copy-start(bf16[128,72,128]{2,1,0:T(8,128)(2,1)S(1)} %all-to-all-done.m_ref) | copy-start | bytes 7077892
  61.7 34.8 %all-to-all-start.1 = ((bf16[128,64,128]{2,1,0:T(8,128)(2,1)}), bf16[128,64,128]{2,1,0:T(8,128)(2,1)S(1)}, u32[]{:S(2)}, u32[]{:S(2)}) async-start(bf16[128,64,128]{2,1,0:T(8,128)(2,1)} %cross_columns.1), calls=%async_computation.1 | async-start | bytes 4194304 | tf_op jit(solution)/shard_map/all_to_all | solution.py:236
  96.5 1.3 %copy-start.1 = (bf16[128,64,128]{2,1,0:T(8,128)(2,1)}, bf16[128,64,128]{2,1,0:T(8,128)(2,1)S(1)}, u32[]{:S(2)}) copy-start(bf16[128,64,128]{2,1,0:T(8,128)(2,1)S(1)} %all-to-all-done.1.m_ref) | copy-start | bytes 6291460
where the time goes:
time: 103 us
  waiting for transfers between devices  64 us (62%)
  Pallas kernels  20.5 us (20%)
  starting transfers between devices  15.3 us (15%)
  local copies, waits for them, and re-layouts  2.74 us (3%)
    all_to_all x1, waiting for transfers between devices, per_device(): moved = lax.all_to_all(sent, AXES, 0, 0, tiled=True)  33.6 us
    all_to_all x1, waiting for transfers between devices, per_device(): returned = lax.all_to_all(crossed, AXES, 0, 0, tiled=True)  30.3 us
    all_to_all x1, starting transfers between devices, per_device(): moved = lax.all_to_all(sent, AXES, 0, 0, tiled=True)  11.5 us
    pallas_call x1, Pallas kernels, per_device(): pl.pallas_call(cross_kernel, grid=(1,), in_specs=[smem, whole(devices, ch...  8.02 us
    pallas_call x1, Pallas kernels, per_device(): pl.pallas_call(forward_kernel, grid=(2,), in_specs=[smem, pl.BlockSpec((2...  7.13 us
    pallas_call x1, Pallas kernels, per_device(): pl.pallas_call(surface_kernel, grid=(SLOTS_HELD,), in_specs=[smem, whole(...  5.31 us
    all_to_all x1, starting transfers between devices, per_device(): returned = lax.all_to_all(crossed, AXES, 0, 0, tiled=True)  3.83 us
    unnamed x4, local copies, waits for them, and re-layouts  2.74 us
  transfers between devices with their start and end apart: 2, of which 2 were waited for; matrix products, arithmetic and copies ran while one was open for 0% of the time, Pallas kernels for 0%

commit v1 on v0

v1 whole, which is shorter than its diff:
```python
import jax
import jax.numpy as jnp
import numpy as np
from jax import lax
from jax.experimental import pallas as pl
from jax.experimental.pallas import tpu as pltpu
from jax.sharding import PartitionSpec as P

AXES = ("scene", "grp")
LENGTH = 512
HALF = LENGTH // 2
SLOTS_HELD = 4
LANES = 128
LANE_BLOCKS = LENGTH // LANES
CHUNK = LANE_BLOCKS * 16
BF16 = jnp.bfloat16
F32 = jnp.float32


def packed_tables(devices):
    places = np.arange(LENGTH)
    packed = LENGTH // devices
    forward = np.zeros((devices, packed, LENGTH))
    backward = np.zeros((devices, packed, LENGTH))
    for dev in range(devices):
        for part in range(packed):
            freq = dev * (packed // 2) + part // 2
            angle = 2.0 * np.pi * ((freq * places) % LENGTH) / LENGTH
            if part % 2 == 0:
                forward[dev, part] = np.cos(angle)
                backward[dev, part] = np.cos(angle) * (1.0 if freq == 0 else 2.0)
            elif freq == 0:
                forward[dev, part] = 1.0 - 2.0 * (places % 2)
                backward[dev, part] = 1.0 - 2.0 * (places % 2)
            else:
                forward[dev, part] = -np.sin(angle)
                backward[dev, part] = -2.0 * np.sin(angle)
    forward = forward.reshape(2, devices // 2, packed, LENGTH).transpose(1, 0, 2, 3)
    forward = forward.reshape(LENGTH, LENGTH)
    backward = backward.reshape(LENGTH, LENGTH).T / LENGTH
    product = places[:, None] * places[None, :] % LENGTH
    cosine = np.cos(2.0 * np.pi * product / LENGTH)
    sine = np.sin(2.0 * np.pi * product / LENGTH)
    packed_sine = np.concatenate([cosine[:, HALF : HALF + 1], sine[:, 1:HALF]], axis=1)
    columns = np.concatenate([cosine[:, :HALF], packed_sine], axis=1)
    columns_back = np.stack([cosine[:HALF], sine[:HALF]])
    columns_back[1, 0] = 0.0
    order = np.arange(4 * 64)
    gather = np.zeros((4 * 64, 4 * 64))
    gather[order, order % 64 * 4 + order // 64] = 1.0
    tables = (forward, backward, columns, columns_back, gather)
    return tuple(jnp.asarray(table.astype(jnp.bfloat16)) for table in tables)


def split_rows(value, rows):
    return value.reshape(value.shape[0] // rows, rows, value.shape[1])


def wide(value):
    return jnp.concatenate([value] * LANE_BLOCKS, axis=1)


def total(value):
    return jnp.sum(jnp.sum(value, axis=0, keepdims=True), axis=1, keepdims=True)


def moments(x_ref, slot):
    rows = 16
    steps = LENGTH // rows
    entries = float(LENGTH * LENGTH)
    base = x_ref[slot, 0:rows, :].astype(F32)
    first = jnp.zeros_like(base)
    second = jnp.zeros_like(base)
    for step in range(1, steps):
        diff = x_ref[slot, step * rows : (step + 1) * rows, :].astype(F32) - base
        first = first + diff
        second = second + diff * diff
    local = base + first * (1.0 / steps)
    mean = total(local) * (steps / entries)
    off = local - mean
    spread = total(second - first * first * (1.0 / steps) + off * off * float(steps))
    return mean, lax.rsqrt(spread * (1.0 / entries) + 1e-05)


def forward_kernel(
    pair_hbm, x_hbm, table_hbm, out_hbm, pair_ref, x_ref, table_ref, out_ref, in_sem, late_sem, out_sem
):
    devices = out_ref.shape[0]
    groups = devices // 2
    blocks = 4
    reads = [pltpu.make_async_copy(x_hbm.at[s], x_ref.at[s], in_sem.at[s]) for s in range(SLOTS_HELD)]
    table_read = pltpu.make_async_copy(table_hbm, table_ref, late_sem.at[0])
    pair_read = pltpu.make_async_copy(pair_hbm, pair_ref, late_sem.at[1])
    reads[0].start()
    table_read.start()
    for read in reads[1:]:
        read.start()
    pair_read.start()
    ones = jnp.ones((LENGTH, LANES), BF16)
    spectra = []
    writes = []
    for s in range(SLOTS_HELD):
        reads[s].wait()
        mean, scale = moments(x_ref, s)
        if s == 0:
            table_read.wait()
            row_sum = jnp.dot(table_ref[...], ones, preferred_element_type=F32)
        product = jnp.dot(table_ref[...], x_ref[s], preferred_element_type=F32)
        spectra.append(split_rows(product * scale - wide(row_sum * (mean * scale)), 8))
        if s % 2 == 0:
            continue
        if s == 1:
            pair_read.wait()
            row = lax.broadcasted_iota(jnp.int32, (8, LANES), 0)
            named = jnp.zeros((8, LANES), F32)
            for column in range(4):
                named = jnp.where(row == column, pair_ref[0, column].astype(F32), named)
            out_ref[:, pl.ds(CHUNK, 8), :] = jnp.broadcast_to(
                named[None], (devices, 8, LANES)
            ).astype(BF16)
        count = groups // blocks
        for block in range(blocks):
            one, two = (part[block * count : (block + 1) * count] for part in spectra[s - 1 :])
            upper = lax.broadcasted_iota(jnp.int32, one.shape, 1) < 4
            low = jnp.where(upper, one, pltpu.roll(two, 4, 1)).astype(BF16)
            high = jnp.where(upper, pltpu.roll(one, 4, 1), two).astype(BF16)
            for side, filled in enumerate((low, high)):
                place = pl.ds(side * groups + block * count, count)
                for lane in range(LANE_BLOCKS):
                    start = lane * 16 + s // 2 * 8
                    out_ref[place, start : start + 8, :] = filled[
                        :, :, lane * LANES : (lane + 1) * LANES
                    ]
                if s == SLOTS_HELD - 1:
                    write = pltpu.make_async_copy(
                        out_ref.at[place], out_hbm.at[place], out_sem.at[2 * block + side]
                    )
                    write.start()
                    writes.append(write)
    for write in writes:
        write.wait()


def take_parts(m_ref, gather, parts_ref):
    for block in range(m_ref.shape[0] // 16):
        rows = jnp.concatenate(
            [
                m_ref[block * 16 : (block + 1) * 16, lane * 16 : (lane + 1) * 16, :].reshape(256, LANES)
                for lane in range(LANE_BLOCKS)
            ],
            axis=1,
        )
        taken = jnp.dot(gather, rows, preferred_element_type=F32).astype(BF16)
        for part in range(4):
            parts_ref[part, block * 64 : (block + 1) * 64, :] = taken[part * 64 : (part + 1) * 64]


def cross(real, imag):
    pairs = real.shape[0] // 2
    own_real, other_real = real[:pairs], real[pairs:]
    own_imag, other_imag = imag[:pairs], imag[pairs:]
    return (
        own_real * other_real + own_imag * other_imag,
        own_imag * other_real - own_real * other_imag,
    )


def cross_kernel(
    first_ref, m_ref, columns_ref, back_ref, gather_ref, out_hbm, parts_ref, names_ref, out_ref, out_sem
):
    devices = m_ref.shape[0]
    slots = devices * SLOTS_HELD
    pairs = devices
    is_first = first_ref[0] == 0

    names_ref[...] = m_ref[:, pl.ds(CHUNK, 8), :].astype(F32).reshape(devices * 8, LANES)
    named = [names_ref[pl.ds(column, devices, stride=8), :] for column in range(4)]
    slot_rows = [
        (named[2 * side] * SLOTS_HELD + named[2 * side + 1]).astype(jnp.int32) for side in range(2)
    ]
    same = lax.broadcasted_iota(jnp.int32, (pairs, LANES), 0) == lax.broadcasted_iota(
        jnp.int32, (pairs, LANES), 1
    )
    slot_lanes = [
        jnp.sum(jnp.where(same, slot_rows[side], 0), axis=0, keepdims=True) for side in range(2)
    ]
    wanted = jnp.concatenate([wide(slot_rows[side]) for side in range(2)], axis=0)
    pick = (wanted == lax.broadcasted_iota(jnp.int32, (2 * pairs, slots), 1)).astype(F32).astype(BF16)
    row = lax.broadcasted_iota(jnp.int32, (devices * 8, 4 * pairs), 0)
    row_code = (row >> 3) * SLOTS_HELD + (row & 3) + ((row >> 2) & 1) * slots
    lane_code = jnp.concatenate(
        [slot_lanes[0], slot_lanes[1], slot_lanes[0] + slots, slot_lanes[1] + slots], axis=1
    )
    place = (row_code == lane_code).astype(F32).astype(BF16)

    take_parts(m_ref, gather_ref[...], parts_ref)

    zero = lax.broadcasted_iota(jnp.int32, (2 * pairs, HALF), 1) == 0
    zero_pairs = lax.broadcasted_iota(jnp.int32, (pairs, HALF), 1) == 0
    sign = (1 - 2 * (lax.broadcasted_iota(jnp.int32, (pairs, LENGTH), 1) & 1)).astype(F32)
    scale = 1.0 / (LENGTH * LENGTH)
    inverse = []
    for freq in range(2):
        products = []
        for part in (2 * freq, 2 * freq + 1):
            picked = jnp.dot(pick, parts_ref[part], preferred_element_type=F32).astype(BF16)
            products.append(jnp.dot(picked, columns_ref[...], preferred_element_type=F32))
        re_cos, re_sin = products[0][:, :HALF], products[0][:, HALF:]
        im_cos, im_sin = products[1][:, :HALF], products[1][:, HALF:]
        re_odd = jnp.where(zero, 0.0, re_sin)
        im_odd = jnp.where(zero, 0.0, im_sin)
        plus = cross(re_cos + im_odd, im_cos - re_odd)
        minus = cross(
            jnp.where(zero, re_sin, re_cos - im_sin), jnp.where(zero, im_sin, im_cos + re_sin)
        )
        if freq == 0:
            low_plus = cross(re_cos, -re_odd)
            low_minus = cross(jnp.where(zero, re_sin, re_cos), re_odd)
            top_plus = cross(im_cos, -im_odd)
            top_minus = cross(jnp.where(zero, im_sin, im_cos), im_odd)
            plus = (
                jnp.where(is_first, low_plus[0] - top_plus[1], plus[0]),
                jnp.where(is_first, low_plus[1] + top_plus[0], plus[1]),
            )
            minus = (
                jnp.where(is_first, low_minus[0] - top_minus[1], minus[0]),
                jnp.where(is_first, low_minus[1] + top_minus[0], minus[1]),
            )
        even = [jnp.where(zero_pairs, plus[k], plus[k] + minus[k]) for k in range(2)]
        odd = [plus[k] - minus[k] for k in range(2)]
        even = jnp.dot(
            jnp.concatenate(even, axis=0).astype(BF16), back_ref[0], preferred_element_type=F32
        )
        odd = jnp.dot(
            jnp.concatenate(odd, axis=0).astype(BF16), back_ref[1], preferred_element_type=F32
        )
        real_cos = even[:pairs] + minus[0][:, :1] * sign
        imag_cos = even[pairs:] + minus[1][:, :1] * sign
        real_sin, imag_sin = odd[:pairs], odd[pairs:]
        own_imag = imag_cos + real_sin
        other_imag = real_sin - imag_cos
        if freq == 0:
            other_imag = jnp.where(is_first, imag_cos - real_sin, other_imag)
        inverse.append(
            (
                jnp.concatenate(
                    [real_cos - imag_sin, real_cos + imag_sin, own_imag, other_imag], axis=0
                )
                * scale
            ).astype(BF16)
        )

    blocks = 4
    count = devices // blocks
    writes = []
    for block in range(blocks):
        rows = place[block * count * 8 : (block + 1) * count * 8]
        placed = [
            split_rows(jnp.dot(rows, inverse[freq], preferred_element_type=F32), 8) for freq in range(2)
        ]
        placed = jnp.concatenate(placed, axis=1).astype(BF16)
        where = pl.ds(block * count, count)
        for lane in range(LANE_BLOCKS):
            out_ref[where, lane * 16 : (lane + 1) * 16, :] = placed[
                :, :, lane * LANES : (lane + 1) * LANES
            ]
        write = pltpu.make_async_copy(out_ref.at[where], out_hbm.at[where], out_sem.at[block])
        write.start()
        writes.append(write)
    for write in writes:
        write.wait()


def surface_kernel(count_ref, m_ref, table_ref, gather_ref, out_hbm, parts_ref, out_ref, out_sem):
    take_parts(m_ref, gather_ref[...], parts_ref)
    writes = []
    for slot in range(SLOTS_HELD):
        keep = (slot < count_ref[0]).astype(F32)
        out_ref[slot] = (
            jnp.dot(table_ref[...], parts_ref[slot], preferred_element_type=F32) * keep
        )
        write = pltpu.make_async_copy(out_ref.at[slot], out_hbm.at[0, slot], out_sem.at[slot])
        write.start()
        writes.append(write)
    for write in writes:
        write.wait()


def per_device(windows, counts, intersection_pairs):
    devices = lax.axis_size(AXES)
    position = lax.axis_index(AXES).astype(jnp.int32).reshape(1)
    forward, backward, columns, columns_back, gather = packed_tables(devices)
    smem = pl.BlockSpec(memory_space=pltpu.SMEM)
    vmem = pl.BlockSpec(memory_space=pltpu.VMEM)
    hbm = pl.BlockSpec(memory_space=pltpu.HBM)
    in_hbm = lambda x: pltpu.with_memory_space_constraint(x, pltpu.HBM)
    dma = pltpu.SemaphoreType.DMA
    params = pltpu.CompilerParams(vmem_limit_bytes=24 << 20)

    sent = pl.pallas_call(
        forward_kernel,
        in_specs=[hbm, hbm, hbm],
        out_specs=hbm,
        out_shape=pltpu.HBM((devices, CHUNK + 8, LANES), BF16),
        scratch_shapes=[
            pltpu.SMEM((1, 4), jnp.int32),
            pltpu.VMEM((SLOTS_HELD, LENGTH, LENGTH), BF16),
            pltpu.VMEM((LENGTH, LENGTH), BF16),
            pltpu.VMEM((devices, CHUNK + 8, LANES), BF16),
            dma((SLOTS_HELD,)),
            dma((2,)),
            dma((8,)),
        ],
        compiler_params=params,
        name="forward_rows",
    )(in_hbm(intersection_pairs), in_hbm(windows[0]), in_hbm(forward))
    moved = lax.all_to_all(sent, AXES, 0, 0, tiled=True)
    crossed = pl.pallas_call(
        cross_kernel,
        in_specs=[smem, vmem, vmem, vmem, vmem],
        out_specs=hbm,
        out_shape=pltpu.HBM((devices, CHUNK, LANES), BF16),
        scratch_shapes=[
            pltpu.VMEM((4, LENGTH, LENGTH), BF16),
            pltpu.VMEM((devices * 8, LANES), F32),
            pltpu.VMEM((devices, CHUNK, LANES), BF16),
            dma((4,)),
        ],
        compiler_params=params,
        name="cross_columns",
    )(position, moved, columns, columns_back, gather)
    returned = lax.all_to_all(crossed, AXES, 0, 0, tiled=True)
    return pl.pallas_call(
        surface_kernel,
        in_specs=[smem, vmem, vmem, vmem],
        out_specs=hbm,
        out_shape=pltpu.HBM((1, SLOTS_HELD, LENGTH, LENGTH), F32),
        scratch_shapes=[
            pltpu.VMEM((SLOTS_HELD, LENGTH, LENGTH), BF16),
            pltpu.VMEM((SLOTS_HELD, LENGTH, LENGTH), F32),
            dma((4,)),
        ],
        compiler_params=params,
        name="surfaces",
    )(counts, returned, backward, gather)


def solution(mesh):
    in_specs = (P(AXES, None, None, None), P(AXES), P(AXES, None))
    out_specs = P(AXES, None, None, None)
    return jax.shard_map(
        per_device, mesh=mesh, in_specs=in_specs, out_specs=out_specs, check_vma=False
    )
```

time: 103 us -> 93.6 us (0.909)
  Pallas kernels: 20.5 us -> 13.2 us
  local copies, waits for them, and re-layouts: 2.74 us -> 0.03 us
    pallas_call x3, Pallas kernels: 20.5 us -> 13.2 us  [the longest x1 5.2 us: per_device(): pl.pallas_call(forward_kernel, in_specs=[hbm, hbm, hbm], out_specs=hbm, o...]
    unnamed x4 -> x8, local copies, waits for them, and re-layouts: 2.74 us -> 0.03 us
where the time goes in v1:
time: 93.6 us; the launch traced here: 93.4 us
  waiting for transfers between devices  64 us (68%)
  starting transfers between devices  15.5 us (17%)
  Pallas kernels  13.2 us (14%)
    all_to_all x1, waiting for transfers between devices, per_device(): moved = lax.all_to_all(sent, AXES, 0, 0, tiled=True)  33.6 us
    all_to_all x1, waiting for transfers between devices, per_device(): returned = lax.all_to_all(crossed, AXES, 0, 0, tiled=True)  30.3 us
    all_to_all x1, starting transfers between devices, per_device(): moved = lax.all_to_all(sent, AXES, 0, 0, tiled=True)  11.5 us
    pallas_call x1, Pallas kernels, per_device(): pl.pallas_call(forward_kernel, in_specs=[hbm, hbm, hbm], out_specs=hbm, o...  5.2 us
    pallas_call x1, Pallas kernels, per_device(): pl.pallas_call(cross_kernel, in_specs=[smem, vmem, vmem, vmem, vmem], out...  4.97 us
    all_to_all x1, starting transfers between devices, per_device(): returned = lax.all_to_all(crossed, AXES, 0, 0, tiled=True)  3.98 us
    pallas_call x1, Pallas kernels, per_device(): pl.pallas_call(surface_kernel, in_specs=[smem, vmem, vmem, vmem], out_spe...  3.03 us
  transfers between devices with their start and end apart: 2, of which 2 were waited for; matrix products, arithmetic and copies ran while one was open for 0% of the time, Pallas kernels for 0%

profile of v1, /device:TPU:1, one launch (start us, length us, event | category | flops | bytes accessed | tf_op | source)
XLA Modules:
  0.0 93.4 jit_solution(17054959898390485258)
XLA Ops:
  0.0 5.2 %forward_rows.1 = bf16[128,72,128]{2,1,0:T(8,128)(2,1)} custom-call(s32[1,4]{1,0:T(1,128)} %pair_hbm.1, bf16[4,512,512]{2,1,0:T(8,128)(2,1)} %bitcast.2, bf16[512,512]{1,0:T(8,128)(2,1)} %constant.21.clone.table_hbm), custom_call_target="tpu_custom_call" | custom-call | tf_op jit(solution)/shard_map/forward_rows/pallas_call | solution.py:300
  5.2 0.0 copy-start
  5.2 0.0 copy-start.1
  5.2 0.0 copy-start.2
  5.2 11.5 %all-to-all-start = ((bf16[128,72,128]{2,1,0:T(8,128)(2,1)}), bf16[128,72,128]{2,1,0:T(8,128)(2,1)S(1)}, u32[]{:S(2)}, u32[]{:S(2)}) async-start(bf16[128,72,128]{2,1,0:T(8,128)(2,1)} %forward_rows.1), calls=%async_computation | async-start | bytes 4718592 | tf_op jit(solution)/shard_map/all_to_all | solution.py:317
  16.8 33.6 %all-to-all-done.m_ref = bf16[128,72,128]{2,1,0:T(8,128)(2,1)S(1)} async-done(((bf16[128,72,128]{2,1,0:T(8,128)(2,1)}), bf16[128,72,128]{2,1,0:T(8,128)(2,1)S(1)}, u32[]{:S(2)}, u32[]{:S(2)}) %all-to-all-start) | async-done | bytes 2359328 | tf_op jit(solution)/shard_map/all_to_all | solution.py:317
  50.4 0.0 copy-done
  50.4 0.0 copy-done.1
  50.4 0.0 copy-done.2
  50.4 5.0 %cross_columns.1 = bf16[128,64,128]{2,1,0:T(8,128)(2,1)} custom-call(s32[1]{0:T(128)} %bitcast.first_ref, bf16[128,72,128]{2,1,0:T(8,128)(2,1)S(1)} %all-to-all-done.m_ref, bf16[512,512]{1,0:T(8,128)(2,1)S(1)} %copy-done.1, bf16[2,256,512]{2,1,0:T(8,128)(2,1)S(1)} %copy-done, bf16[256,256]{1,0:T(8,128)(2,1)S(1)} %copy-done.2), custom_call_target="tpu_custom_call" | custom-call | tf_op jit(solution)/shard_map/cross_columns/pallas_call | solution.py:318
  55.4 0.0 copy-start.3
  55.4 4.0 %all-to-all-start.1 = ((bf16[128,64,128]{2,1,0:T(8,128)(2,1)}), bf16[128,64,128]{2,1,0:T(8,128)(2,1)S(1)}, u32[]{:S(2)}, u32[]{:S(2)}) async-start(bf16[128,64,128]{2,1,0:T(8,128)(2,1)} %cross_columns.1), calls=%async_computation.1 | async-start | bytes 4194304 | tf_op jit(solution)/shard_map/all_to_all | solution.py:332
  60.0 30.3 %all-to-all-done.1.m_ref = bf16[128,64,128]{2,1,0:T(8,128)(2,1)S(1)} async-done(((bf16[128,64,128]{2,1,0:T(8,128)(2,1)}), bf16[128,64,128]{2,1,0:T(8,128)(2,1)S(1)}, u32[]{:S(2)}, u32[]{:S(2)}) %all-to-all-start.1) | async-done | bytes 2097184 | tf_op jit(solution)/shard_map/all_to_all | solution.py:332
  90.4 0.0 copy-done.3
  90.4 3.0 %surfaces.1 = f32[1,4,512,512]{3,2,1,0:T(8,128)} custom-call(s32[1]{0:T(128)S(6)} %copy.9.count_ref, bf16[128,64,128]{2,1,0:T(8,128)(2,1)S(1)} %all-to-all-done.1.m_ref, bf16[512,512]{1,0:T(8,128)(2,1)S(1)} %copy-done.3, bf16[256,256]{1,0:T(8,128)(2,1)S(1)} %copy-done.2), custom_call_target="tpu_custom_call" | custom-call | tf_op jit(solution)/shard_map/surfaces/pallas_call | solution.py:333
Async XLA Ops:
  5.2 45.2 %copy-start = (bf16[2,256,512]{2,1,0:T(8,128)(2,1)S(1)}, bf16[2,256,512]{2,1,0:T(8,128)(2,1)}, u32[]{:S(2)}) copy-start(bf16[2,256,512]{2,1,0:T(8,128)(2,1)} %constant.24.clone.back_ref) | copy-start | bytes 1572868
  5.2 45.2 %copy-start.1 = (bf16[512,512]{1,0:T(8,128)(2,1)S(1)}, bf16[512,512]{1,0:T(8,128)(2,1)}, u32[]{:S(2)}) copy-start(bf16[512,512]{1,0:T(8,128)(2,1)} %constant.23.clone.columns_ref) | copy-start | bytes 1572868
  5.2 45.2 %copy-start.2 = (bf16[256,256]{1,0:T(8,128)(2,1)S(1)}, bf16[256,256]{1,0:T(8,128)(2,1)}, u32[]{:S(2)}) copy-start(bf16[256,256]{1,0:T(8,128)(2,1)} %constant.25.clone.gather_ref) | copy-start | bytes 393220
  5.2 45.2 %all-to-all-start = ((bf16[128,72,128]{2,1,0:T(8,128)(2,1)}), bf16[128,72,128]{2,1,0:T(8,128)(2,1)S(1)}, u32[]{:S(2)}, u32[]{:S(2)}) async-start(bf16[128,72,128]{2,1,0:T(8,128)(2,1)} %forward_rows.1), calls=%async_computation | async-start | bytes 4718592 | tf_op jit(solution)/shard_map/all_to_all | solution.py:317
  55.4 35.0 %copy-start.3 = (bf16[512,512]{1,0:T(8,128)(2,1)S(1)}, bf16[512,512]{1,0:T(8,128)(2,1)}, u32[]{:S(2)}) copy-start(bf16[512,512]{1,0:T(8,128)(2,1)} %constant.22.clone.table_ref) | copy-start | bytes 1572868
  55.4 35.0 %all-to-all-start.1 = ((bf16[128,64,128]{2,1,0:T(8,128)(2,1)}), bf16[128,64,128]{2,1,0:T(8,128)(2,1)S(1)}, u32[]{:S(2)}, u32[]{:S(2)}) async-start(bf16[128,64,128]{2,1,0:T(8,128)(2,1)} %cross_columns.1), calls=%async_computation.1 | async-start | bytes 4194304 | tf_op jit(solution)/shard_map/all_to_all | solution.py:332

commit v2 on v1

--- a/solution.py
+++ b/solution.py
@@ -13,6 +13,7 @@
 LANES = 128
 LANE_BLOCKS = LENGTH // LANES
 CHUNK = LANE_BLOCKS * 16
+TILES = CHUNK // 2 + 1
 BF16 = jnp.bfloat16
 F32 = jnp.float32
 
@@ -48,7 +49,10 @@
     order = np.arange(4 * 64)
     gather = np.zeros((4 * 64, 4 * 64))
     gather[order, order % 64 * 4 + order // 64] = 1.0
-    tables = (forward, backward, columns, columns_back, gather)
+    dev, slot, part = order % 64 // 4, order % 4, order // 64
+    gather_slots = np.zeros((4 * 64, 4 * 64))
+    gather_slots[order, slot // 2 * 128 + dev * 8 + slot % 2 * 4 + part] = 1.0
+    tables = (forward, backward, columns, columns_back, gather_slots, gather)
     return tuple(jnp.asarray(table.astype(jnp.bfloat16)) for table in tables)
 
 
@@ -83,11 +87,23 @@
 
 
 def forward_kernel(
-    pair_hbm, x_hbm, table_hbm, out_hbm, pair_ref, x_ref, table_ref, out_ref, in_sem, late_sem, out_sem
+    pair_hbm,
+    x_hbm,
+    table_hbm,
+    out_hbm,
+    pair_ref,
+    x_ref,
+    table_ref,
+    out_ref,
+    names_ref,
+    in_sem,
+    late_sem,
+    out_sem,
 ):
     devices = out_ref.shape[0]
     groups = devices // 2
     blocks = 4
+    out_rows = out_hbm.reshape(devices, 2 * TILES, LANES)
     reads = [pltpu.make_async_copy(x_hbm.at[s], x_ref.at[s], in_sem.at[s]) for s in range(SLOTS_HELD)]
     table_read = pltpu.make_async_copy(table_hbm, table_ref, late_sem.at[0])
     pair_read = pltpu.make_async_copy(pair_hbm, pair_ref, late_sem.at[1])
@@ -111,13 +127,14 @@
             continue
         if s == 1:
             pair_read.wait()
-            row = lax.broadcasted_iota(jnp.int32, (8, LANES), 0)
-            named = jnp.zeros((8, LANES), F32)
-            for column in range(4):
-                named = jnp.where(row == column, pair_ref[0, column].astype(F32), named)
-            out_ref[:, pl.ds(CHUNK, 8), :] = jnp.broadcast_to(
-                named[None], (devices, 8, LANES)
-            ).astype(BF16)
+            column = lax.broadcasted_iota(jnp.int32, (2, LANES), 1) // (LANES // 4)
+            named = jnp.zeros((2, LANES), F32)
+            for k in range(4):
+                named = jnp.where(column == k, pair_ref[0, k].astype(F32), named)
+            names_ref[...] = jnp.broadcast_to(named[None], (devices, 2, LANES)).astype(BF16)
+            write = pltpu.make_async_copy(names_ref, out_hbm.at[:, TILES - 1], late_sem.at[2])
+            write.start()
+            writes.append(write)
         count = groups // blocks
         for block in range(blocks):
             one, two = (part[block * count : (block + 1) * count] for part in spectra[s - 1 :])
@@ -127,29 +144,47 @@
             for side, filled in enumerate((low, high)):
                 place = pl.ds(side * groups + block * count, count)
                 for lane in range(LANE_BLOCKS):
-                    start = lane * 16 + s // 2 * 8
-                    out_ref[place, start : start + 8, :] = filled[
-                        :, :, lane * LANES : (lane + 1) * LANES
-                    ]
-                if s == SLOTS_HELD - 1:
-                    write = pltpu.make_async_copy(
-                        out_ref.at[place], out_hbm.at[place], out_sem.at[2 * block + side]
-                    )
-                    write.start()
-                    writes.append(write)
+                    start = s // 2 * 32 + lane * 8
+                    out_ref[place, start : start + 8] = filled[:, :, lane * LANES : (lane + 1) * LANES]
+                rows = pl.ds(s // 2 * 32, 32)
+                write = pltpu.make_async_copy(
+                    out_ref.at[place, rows], out_rows.at[place, rows], out_sem.at[s // 2, 2 * block + side]
+                )
+                write.start()
+                writes.append(write)
     for write in writes:
         write.wait()
 
 
-def take_parts(m_ref, gather, parts_ref):
+def rows_of_16(m_ref, block):
+    return jnp.concatenate(
+        [
+            m_ref[block * 16 : (block + 1) * 16, lane * 16 : (lane + 1) * 16, :].reshape(256, LANES)
+            for lane in range(LANE_BLOCKS)
+        ],
+        axis=1,
+    )
+
+
+def rows_of_8(rows_ref, block):
+    tile = lambda k: (
+        rows_ref[block * 16 : (block + 1) * 16, k * 8 : (k + 1) * 8]
+        .astype(F32)
+        .reshape(128, LANES)
+        .astype(BF16)
+    )
+    return jnp.concatenate(
+        [
+            jnp.concatenate([tile(lane), tile(LANE_BLOCKS + lane)], axis=0)
+            for lane in range(LANE_BLOCKS)
+        ],
+        axis=1,
+    )
+
+
+def take_parts(m_ref, rows_of, gather, parts_ref):
     for block in range(m_ref.shape[0] // 16):
-        rows = jnp.concatenate(
-            [
-                m_ref[block * 16 : (block + 1) * 16, lane * 16 : (lane + 1) * 16, :].reshape(256, LANES)
-                for lane in range(LANE_BLOCKS)
-            ],
-            axis=1,
-        )
+        rows = rows_of(m_ref, block)
         taken = jnp.dot(gather, rows, preferred_element_type=F32).astype(BF16)
         for part in range(4):
             parts_ref[part, block * 64 : (block + 1) * 64, :] = taken[part * 64 : (part + 1) * 64]
@@ -166,15 +201,24 @@
 
 
 def cross_kernel(
-    first_ref, m_ref, columns_ref, back_ref, gather_ref, out_hbm, parts_ref, names_ref, out_ref, out_sem
+    first_ref, m_ref, columns_ref, back_ref, gather_ref, out_hbm, rows_ref, parts_ref, names_ref,
+    out_ref, in_sem, out_sem
 ):
     devices = m_ref.shape[0]
     slots = devices * SLOTS_HELD
     pairs = devices
     is_first = first_ref[0] == 0
 
-    names_ref[...] = m_ref[:, pl.ds(CHUNK, 8), :].astype(F32).reshape(devices * 8, LANES)
-    named = [names_ref[pl.ds(column, devices, stride=8), :] for column in range(4)]
+    copy = pltpu.make_async_copy(
+        m_ref.reshape(devices, 2 * TILES, LANES).at[:, 0:CHUNK], rows_ref, in_sem.at[0]
+    )
+    copy.start()
+    names_ref[...] = m_ref[:, TILES - 1].astype(F32).reshape(devices * 2, LANES)
+    names = names_ref[pl.ds(0, devices, stride=2), :]
+    named = [
+        jnp.broadcast_to(names[:, k * LANES // 4 : k * LANES // 4 + 1], (devices, LANES))
+        for k in range(4)
+    ]
     slot_rows = [
         (named[2 * side] * SLOTS_HELD + named[2 * side + 1]).astype(jnp.int32) for side in range(2)
     ]
@@ -186,25 +230,34 @@
     ]
     wanted = jnp.concatenate([wide(slot_rows[side]) for side in range(2)], axis=0)
     pick = (wanted == lax.broadcasted_iota(jnp.int32, (2 * pairs, slots), 1)).astype(F32).astype(BF16)
-    row = lax.broadcasted_iota(jnp.int32, (devices * 8, 4 * pairs), 0)
-    row_code = (row >> 3) * SLOTS_HELD + (row & 3) + ((row >> 2) & 1) * slots
-    lane_code = jnp.concatenate(
-        [slot_lanes[0], slot_lanes[1], slot_lanes[0] + slots, slot_lanes[1] + slots], axis=1
-    )
-    place = (row_code == lane_code).astype(F32).astype(BF16)
-
-    take_parts(m_ref, gather_ref[...], parts_ref)
+    group = lax.broadcasted_iota(jnp.int32, (devices, 8, LANES), 0)
+    inner = lax.broadcasted_iota(jnp.int32, (devices, 8, LANES), 1)
+    row_code = (group * SLOTS_HELD + ((inner & 3) + (inner >> 2) * slots)).reshape(devices * 8, LANES)
+    place = jnp.concatenate(
+        [
+            (row_code == slot_lanes[side] + part * slots).astype(F32).astype(BF16)
+            for part in range(2)
+            for side in range(2)
+        ],
+        axis=1,
+    )
+    copy.wait()
+    take_parts(rows_ref, rows_of_8, gather_ref[...], parts_ref)
 
     zero = lax.broadcasted_iota(jnp.int32, (2 * pairs, HALF), 1) == 0
     zero_pairs = lax.broadcasted_iota(jnp.int32, (pairs, HALF), 1) == 0
     sign = (1 - 2 * (lax.broadcasted_iota(jnp.int32, (pairs, LENGTH), 1) & 1)).astype(F32)
     scale = 1.0 / (LENGTH * LENGTH)
+    picked = [
+        jnp.dot(pick, parts_ref[part], preferred_element_type=F32).astype(BF16) for part in range(4)
+    ]
     inverse = []
     for freq in range(2):
         products = []
         for part in (2 * freq, 2 * freq + 1):
-            picked = jnp.dot(pick, parts_ref[part], preferred_element_type=F32).astype(BF16)
-            products.append(jnp.dot(picked, columns_ref[...], preferred_element_type=F32))
+            products.append(
+                jnp.dot(picked[part], columns_ref[...], preferred_element_type=F32)
+            )
         re_cos, re_sin = products[0][:, :HALF], products[0][:, HALF:]
         im_cos, im_sin = products[1][:, :HALF], products[1][:, HALF:]
         re_odd = jnp.where(zero, 0.0, re_sin)
@@ -272,7 +325,7 @@
 
 
 def surface_kernel(count_ref, m_ref, table_ref, gather_ref, out_hbm, parts_ref, out_ref, out_sem):
-    take_parts(m_ref, gather_ref[...], parts_ref)
+    take_parts(m_ref, rows_of_16, gather_ref[...], parts_ref)
     writes = []
     for slot in range(SLOTS_HELD):
         keep = (slot < count_ref[0]).astype(F32)
@@ -289,7 +342,7 @@
 def per_device(windows, counts, intersection_pairs):
     devices = lax.axis_size(AXES)
     position = lax.axis_index(AXES).astype(jnp.int32).reshape(1)
-    forward, backward, columns, columns_back, gather = packed_tables(devices)
+    forward, backward, columns, columns_back, gather_slots, gather = packed_tables(devices)
     smem = pl.BlockSpec(memory_space=pltpu.SMEM)
     vmem = pl.BlockSpec(memory_space=pltpu.VMEM)
     hbm = pl.BlockSpec(memory_space=pltpu.HBM)
@@ -301,15 +354,16 @@
         forward_kernel,
         in_specs=[hbm, hbm, hbm],
         out_specs=hbm,
-        out_shape=pltpu.HBM((devices, CHUNK + 8, LANES), BF16),
+        out_shape=pltpu.HBM((devices, TILES, 2, LANES), BF16),
         scratch_shapes=[
             pltpu.SMEM((1, 4), jnp.int32),
             pltpu.VMEM((SLOTS_HELD, LENGTH, LENGTH), BF16),
             pltpu.VMEM((LENGTH, LENGTH), BF16),
-            pltpu.VMEM((devices, CHUNK + 8, LANES), BF16),
+            pltpu.VMEM((devices, CHUNK, LANES), BF16),
+            pltpu.VMEM((devices, 2, LANES), BF16),
             dma((SLOTS_HELD,)),
-            dma((2,)),
-            dma((8,)),
+            dma((3,)),
+            dma((2, 8)),
         ],
         compiler_params=params,
         name="forward_rows",
@@ -321,14 +375,16 @@
         out_specs=hbm,
         out_shape=pltpu.HBM((devices, CHUNK, LANES), BF16),
         scratch_shapes=[
+            pltpu.VMEM((devices, CHUNK, LANES), BF16),
             pltpu.VMEM((4, LENGTH, LENGTH), BF16),
-            pltpu.VMEM((devices * 8, LANES), F32),
+            pltpu.VMEM((devices * 2, LANES), F32),
             pltpu.VMEM((devices, CHUNK, LANES), BF16),
+            dma((1,)),
             dma((4,)),
         ],
         compiler_params=params,
         name="cross_columns",
-    )(position, moved, columns, columns_back, gather)
+    )(position, moved, columns, columns_back, gather_slots)
     returned = lax.all_to_all(crossed, AXES, 0, 0, tiled=True)
     return pl.pallas_call(
         surface_kernel,

time: 93.6 us -> 91.7 us (0.980)
  waiting for transfers between devices: 64 us -> 61.8 us
    all_to_all x1, waiting for transfers between devices: 33.6 us -> 31.5 us  [per_device(): moved = lax.all_to_all(sent, AXES, 0, 0, tiled=True)]
where the time goes in v2:
time: 91.7 us; the launch traced here: 91.4 us
  waiting for transfers between devices  61.8 us (67%)
  starting transfers between devices  15.5 us (17%)
  Pallas kernels  13.3 us (15%)
    all_to_all x1, waiting for transfers between devices, per_device(): moved = lax.all_to_all(sent, AXES, 0, 0, tiled=True)  31.5 us
    all_to_all x1, waiting for transfers between devices, per_device(): returned = lax.all_to_all(crossed, AXES, 0, 0, tiled=True)  30.3 us
    all_to_all x1, starting transfers between devices, per_device(): moved = lax.all_to_all(sent, AXES, 0, 0, tiled=True)  11.5 us
    pallas_call x1, Pallas kernels, per_device(): pl.pallas_call(cross_kernel, in_specs=[smem, vmem, vmem, vmem, vmem], out...  5.41 us
    pallas_call x1, Pallas kernels, per_device(): pl.pallas_call(forward_kernel, in_specs=[hbm, hbm, hbm], out_specs=hbm, o...  4.88 us
    all_to_all x1, starting transfers between devices, per_device(): returned = lax.all_to_all(crossed, AXES, 0, 0, tiled=True)  3.99 us
    pallas_call x1, Pallas kernels, per_device(): pl.pallas_call(surface_kernel, in_specs=[smem, vmem, vmem, vmem], out_spe...  3.03 us
  transfers between devices with their start and end apart: 2, of which 2 were waited for; matrix products, arithmetic and copies ran while one was open for 0% of the time, Pallas kernels for 0%

profile of v2, /device:TPU:1, one launch (start us, length us, event | category | flops | bytes accessed | tf_op | source)
XLA Modules:
  0.0 91.4 jit_solution(17236984872932860080)
XLA Ops:
  0.0 4.9 %forward_rows.1 = bf16[128,33,2,128]{3,2,1,0:T(2,128)(2,1)} custom-call(s32[1,4]{1,0:T(1,128)} %pair_hbm.1, bf16[4,512,512]{2,1,0:T(8,128)(2,1)} %bitcast.2, bf16[512,512]{1,0:T(8,128)(2,1)} %constant.23.clone.table_hbm), custom_call_target="tpu_custom_call" | custom-call | tf_op jit(solution)/shard_map/forward_rows/pallas_call | solution.py:353
  4.9 0.0 copy-start.1
  4.9 0.0 copy-start.2
  4.9 0.0 copy-start.4
  4.9 11.5 %all-to-all-start = ((bf16[128,33,2,128]{3,2,1,0:T(2,128)(2,1)}), bf16[128,33,2,128]{3,2,1,0:T(2,128)(2,1)S(1)}, u32[]{:S(2)}, u32[]{:S(2)}) async-start(bf16[128,33,2,128]{3,2,1,0:T(2,128)(2,1)} %forward_rows.1), calls=%async_computation | async-start | bytes 4325376 | tf_op jit(solution)/shard_map/all_to_all | solution.py:371
  16.4 31.5 %all-to-all-done.m_ref = bf16[128,33,2,128]{3,2,1,0:T(2,128)(2,1)S(1)} async-done(((bf16[128,33,2,128]{3,2,1,0:T(2,128)(2,1)}), bf16[128,33,2,128]{3,2,1,0:T(2,128)(2,1)S(1)}, u32[]{:S(2)}, u32[]{:S(2)}) %all-to-all-start) | async-done | bytes 2162720 | tf_op jit(solution)/shard_map/all_to_all | solution.py:371
  48.0 0.0 copy-done.1
  48.0 0.0 copy-done.2
  48.0 0.0 copy-done.4
  48.0 5.4 %cross_columns.1 = bf16[128,64,128]{2,1,0:T(8,128)(2,1)} custom-call(s32[1]{0:T(128)} %bitcast.first_ref, bf16[128,33,2,128]{3,2,1,0:T(2,128)(2,1)S(1)} %all-to-all-done.m_ref, bf16[512,512]{1,0:T(8,128)(2,1)S(1)} %copy-done.2, bf16[2,256,512]{2,1,0:T(8,128)(2,1)S(1)} %copy-done.1, bf16[256,256]{1,0:T(8,128)(2,1)S(1)} %copy-done.4), custom_call_target="tpu_custom_call" | custom-call | tf_op jit(solution)/shard_map/cross_columns/pallas_call | solution.py:372
  53.4 0.0 copy-start
  53.4 0.0 copy-start.3
  53.4 4.0 %all-to-all-start.1 = ((bf16[128,64,128]{2,1,0:T(8,128)(2,1)}), bf16[128,64,128]{2,1,0:T(8,128)(2,1)S(1)}, u32[]{:S(2)}, u32[]{:S(2)}) async-start(bf16[128,64,128]{2,1,0:T(8,128)(2,1)} %cross_columns.1), calls=%async_computation.1 | async-start | bytes 4194304 | tf_op jit(solution)/shard_map/all_to_all | solution.py:388
  58.1 30.3 %all-to-all-done.1.m_ref = bf16[128,64,128]{2,1,0:T(8,128)(2,1)S(1)} async-done(((bf16[128,64,128]{2,1,0:T(8,128)(2,1)}), bf16[128,64,128]{2,1,0:T(8,128)(2,1)S(1)}, u32[]{:S(2)}, u32[]{:S(2)}) %all-to-all-start.1) | async-done | bytes 2097184 | tf_op jit(solution)/shard_map/all_to_all | solution.py:388
  88.4 0.0 copy-done
  88.4 0.0 copy-done.3
  88.4 3.0 %surfaces.1 = f32[1,4,512,512]{3,2,1,0:T(8,128)} custom-call(s32[1]{0:T(128)S(6)} %copy.10.count_ref, bf16[128,64,128]{2,1,0:T(8,128)(2,1)S(1)} %all-to-all-done.1.m_ref, bf16[512,512]{1,0:T(8,128)(2,1)S(1)} %copy-done, bf16[256,256]{1,0:T(8,128)(2,1)S(1)} %copy-done.3), custom_call_target="tpu_custom_call" | custom-call | tf_op jit(solution)/shard_map/surfaces/pallas_call | solution.py:389
Async XLA Ops:
  4.9 43.1 %copy-start.1 = (bf16[2,256,512]{2,1,0:T(8,128)(2,1)S(1)}, bf16[2,256,512]{2,1,0:T(8,128)(2,1)}, u32[]{:S(2)}) copy-start(bf16[2,256,512]{2,1,0:T(8,128)(2,1)} %constant.26.clone.back_ref) | copy-start | bytes 1572868
  4.9 43.1 %copy-start.2 = (bf16[512,512]{1,0:T(8,128)(2,1)S(1)}, bf16[512,512]{1,0:T(8,128)(2,1)}, u32[]{:S(2)}) copy-start(bf16[512,512]{1,0:T(8,128)(2,1)} %constant.25.clone.columns_ref) | copy-start | bytes 1572868
  4.9 43.1 %copy-start.4 = (bf16[256,256]{1,0:T(8,128)(2,1)S(1)}, bf16[256,256]{1,0:T(8,128)(2,1)}, u32[]{:S(2)}) copy-start(bf16[256,256]{1,0:T(8,128)(2,1)} %constant.27.clone.gather_ref) | copy-start | bytes 393220
  4.9 43.0 %all-to-all-start = ((bf16[128,33,2,128]{3,2,1,0:T(2,128)(2,1)}), bf16[128,33,2,128]{3,2,1,0:T(2,128)(2,1)S(1)}, u32[]{:S(2)}, u32[]{:S(2)}) async-start(bf16[128,33,2,128]{3,2,1,0:T(2,128)(2,1)} %forward_rows.1), calls=%async_computation | async-start | bytes 4325376 | tf_op jit(solution)/shard_map/all_to_all | solution.py:371
  53.4 35.0 %copy-start = (bf16[512,512]{1,0:T(8,128)(2,1)S(1)}, bf16[512,512]{1,0:T(8,128)(2,1)}, u32[]{:S(2)}) copy-start(bf16[512,512]{1,0:T(8,128)(2,1)} %constant.24.clone.table_ref) | copy-start | bytes 1572868
  53.4 35.0 %copy-start.3 = (bf16[256,256]{1,0:T(8,128)(2,1)S(1)}, bf16[256,256]{1,0:T(8,128)(2,1)}, u32[]{:S(2)}) copy-start(bf16[256,256]{1,0:T(8,128)(2,1)} %constant.28.clone.gather_ref) | copy-start | bytes 393220
  53.4 35.0 %all-to-all-start.1 = ((bf16[128,64,128]{2,1,0:T(8,128)(2,1)}), bf16[128,64,128]{2,1,0:T(8,128)(2,1)S(1)}, u32[]{:S(2)}, u32[]{:S(2)}) async-start(bf16[128,64,128]{2,1,0:T(8,128)(2,1)} %cross_columns.1), calls=%async_computation.1 | async-start | bytes 4194304 | tf_op jit(solution)/shard_map/all_to_all | solution.py:388

commit v3 on v2

--- a/solution.py
+++ b/solution.py
@@ -102,7 +102,7 @@
 ):
     devices = out_ref.shape[0]
     groups = devices // 2
-    blocks = 4
+    blocks = 8
     out_rows = out_hbm.reshape(devices, 2 * TILES, LANES)
     reads = [pltpu.make_async_copy(x_hbm.at[s], x_ref.at[s], in_sem.at[s]) for s in range(SLOTS_HELD)]
     table_read = pltpu.make_async_copy(table_hbm, table_ref, late_sem.at[0])
@@ -251,13 +251,14 @@
     picked = [
         jnp.dot(pick, parts_ref[part], preferred_element_type=F32).astype(BF16) for part in range(4)
     ]
+    spectra = jnp.dot(
+        jnp.concatenate(picked, axis=0), columns_ref[...], preferred_element_type=F32
+    )
     inverse = []
     for freq in range(2):
-        products = []
-        for part in (2 * freq, 2 * freq + 1):
-            products.append(
-                jnp.dot(picked[part], columns_ref[...], preferred_element_type=F32)
-            )
+        products = [
+            spectra[part * 2 * pairs : (part + 1) * 2 * pairs] for part in (2 * freq, 2 * freq + 1)
+        ]
         re_cos, re_sin = products[0][:, :HALF], products[0][:, HALF:]
         im_cos, im_sin = products[1][:, :HALF], products[1][:, HALF:]
         re_odd = jnp.where(zero, 0.0, re_sin)
@@ -327,14 +328,19 @@
 def surface_kernel(count_ref, m_ref, table_ref, gather_ref, out_hbm, parts_ref, out_ref, out_sem):
     take_parts(m_ref, rows_of_16, gather_ref[...], parts_ref)
     writes = []
+    parts = 2
     for slot in range(SLOTS_HELD):
         keep = (slot < count_ref[0]).astype(F32)
-        out_ref[slot] = (
-            jnp.dot(table_ref[...], parts_ref[slot], preferred_element_type=F32) * keep
-        )
-        write = pltpu.make_async_copy(out_ref.at[slot], out_hbm.at[0, slot], out_sem.at[slot])
-        write.start()
-        writes.append(write)
+        for part in range(parts):
+            rows = pl.ds(part * LENGTH // parts, LENGTH // parts)
+            out_ref[slot, rows] = (
+                jnp.dot(table_ref[rows], parts_ref[slot], preferred_element_type=F32) * keep
+            )
+            write = pltpu.make_async_copy(
+                out_ref.at[slot, rows], out_hbm.at[0, slot, rows], out_sem.at[slot, part]
+            )
+            write.start()
+            writes.append(write)
     for write in writes:
         write.wait()
 
@@ -363,7 +369,7 @@
             pltpu.VMEM((devices, 2, LANES), BF16),
             dma((SLOTS_HELD,)),
             dma((3,)),
-            dma((2, 8)),
+            dma((2, 16)),
         ],
         compiler_params=params,
         name="forward_rows",
@@ -394,7 +400,7 @@
         scratch_shapes=[
             pltpu.VMEM((SLOTS_HELD, LENGTH, LENGTH), BF16),
             pltpu.VMEM((SLOTS_HELD, LENGTH, LENGTH), F32),
-            dma((4,)),
+            dma((4, 2)),
         ],
         compiler_params=params,
         name="surfaces",

time: 91.7 us -> 91.5 us (level)
  no operation moved by 1% of the time
where the time goes in v3:
time: 91.5 us; the launch traced here: 91.2 us
  waiting for transfers between devices  61.8 us (68%)
  starting transfers between devices  15.5 us (17%)
  Pallas kernels  13.1 us (14%)
    all_to_all x1, waiting for transfers between devices, per_device(): moved = lax.all_to_all(sent, AXES, 0, 0, tiled=True)  31.5 us
    all_to_all x1, waiting for transfers between devices, per_device(): returned = lax.all_to_all(crossed, AXES, 0, 0, tiled=True)  30.3 us
    all_to_all x1, starting transfers between devices, per_device(): moved = lax.all_to_all(sent, AXES, 0, 0, tiled=True)  11.5 us
    pallas_call x1, Pallas kernels, per_device(): pl.pallas_call(cross_kernel, in_specs=[smem, vmem, vmem, vmem, vmem], out...  5.28 us
    pallas_call x1, Pallas kernels, per_device(): pl.pallas_call(forward_kernel, in_specs=[hbm, hbm, hbm], out_specs=hbm, o...  4.93 us
    all_to_all x1, starting transfers between devices, per_device(): returned = lax.all_to_all(crossed, AXES, 0, 0, tiled=True)  4 us
    pallas_call x1, Pallas kernels, per_device(): pl.pallas_call(surface_kernel, in_specs=[smem, vmem, vmem, vmem], out_spe...  2.92 us
  transfers between devices with their start and end apart: 2, of which 2 were waited for; matrix products, arithmetic and copies ran while one was open for 0% of the time, Pallas kernels for 0%

profile of v3, /device:TPU:1, one launch (start us, length us, event | category | flops | bytes accessed | tf_op | source)
XLA Modules:
  0.0 91.2 jit_solution(12370750644893929074)
XLA Ops:
  0.0 4.9 %forward_rows.1 = bf16[128,33,2,128]{3,2,1,0:T(2,128)(2,1)} custom-call(s32[1,4]{1,0:T(1,128)} %pair_hbm.1, bf16[4,512,512]{2,1,0:T(8,128)(2,1)} %bitcast.2, bf16[512,512]{1,0:T(8,128)(2,1)} %constant.23.clone.table_hbm), custom_call_target="tpu_custom_call" | custom-call | tf_op jit(solution)/shard_map/forward_rows/pallas_call | solution.py:359
  4.9 0.0 copy-start.1
  4.9 0.0 copy-start.2
  5.0 0.0 copy-start.4
  5.0 11.5 %all-to-all-start = ((bf16[128,33,2,128]{3,2,1,0:T(2,128)(2,1)}), bf16[128,33,2,128]{3,2,1,0:T(2,128)(2,1)S(1)}, u32[]{:S(2)}, u32[]{:S(2)}) async-start(bf16[128,33,2,128]{3,2,1,0:T(2,128)(2,1)} %forward_rows.1), calls=%async_computation | async-start | bytes 4325376 | tf_op jit(solution)/shard_map/all_to_all | solution.py:377
  16.5 31.5 %all-to-all-done.m_ref = bf16[128,33,2,128]{3,2,1,0:T(2,128)(2,1)S(1)} async-done(((bf16[128,33,2,128]{3,2,1,0:T(2,128)(2,1)}), bf16[128,33,2,128]{3,2,1,0:T(2,128)(2,1)S(1)}, u32[]{:S(2)}, u32[]{:S(2)}) %all-to-all-start) | async-done | bytes 2162720 | tf_op jit(solution)/shard_map/all_to_all | solution.py:377
  48.0 0.0 copy-done.1
  48.0 0.0 copy-done.2
  48.0 0.0 copy-done.4
  48.0 5.3 %cross_columns.1 = bf16[128,64,128]{2,1,0:T(8,128)(2,1)} custom-call(s32[1]{0:T(128)} %bitcast.first_ref, bf16[128,33,2,128]{3,2,1,0:T(2,128)(2,1)S(1)} %all-to-all-done.m_ref, bf16[512,512]{1,0:T(8,128)(2,1)S(1)} %copy-done.2, bf16[2,256,512]{2,1,0:T(8,128)(2,1)S(1)} %copy-done.1, bf16[256,256]{1,0:T(8,128)(2,1)S(1)} %copy-done.4), custom_call_target="tpu_custom_call" | custom-call | tf_op jit(solution)/shard_map/cross_columns/pallas_call | solution.py:378
  53.3 0.0 copy-start
  53.3 0.0 copy-start.3
  53.3 4.0 %all-to-all-start.1 = ((bf16[128,64,128]{2,1,0:T(8,128)(2,1)}), bf16[128,64,128]{2,1,0:T(8,128)(2,1)S(1)}, u32[]{:S(2)}, u32[]{:S(2)}) async-start(bf16[128,64,128]{2,1,0:T(8,128)(2,1)} %cross_columns.1), calls=%async_computation.1 | async-start | bytes 4194304 | tf_op jit(solution)/shard_map/all_to_all | solution.py:394
  58.0 30.3 %all-to-all-done.1.m_ref = bf16[128,64,128]{2,1,0:T(8,128)(2,1)S(1)} async-done(((bf16[128,64,128]{2,1,0:T(8,128)(2,1)}), bf16[128,64,128]{2,1,0:T(8,128)(2,1)S(1)}, u32[]{:S(2)}, u32[]{:S(2)}) %all-to-all-start.1) | async-done | bytes 2097184 | tf_op jit(solution)/shard_map/all_to_all | solution.py:394
  88.3 0.0 copy-done
  88.3 0.0 copy-done.3
  88.3 2.9 %surfaces.1 = f32[1,4,512,512]{3,2,1,0:T(8,128)} custom-call(s32[1]{0:T(128)S(6)} %copy.10.count_ref, bf16[128,64,128]{2,1,0:T(8,128)(2,1)S(1)} %all-to-all-done.1.m_ref, bf16[512,512]{1,0:T(8,128)(2,1)S(1)} %copy-done, bf16[256,256]{1,0:T(8,128)(2,1)S(1)} %copy-done.3), custom_call_target="tpu_custom_call" | custom-call | tf_op jit(solution)/shard_map/surfaces/pallas_call | solution.py:395
Async XLA Ops:
  4.9 43.1 %copy-start.1 = (bf16[2,256,512]{2,1,0:T(8,128)(2,1)S(1)}, bf16[2,256,512]{2,1,0:T(8,128)(2,1)}, u32[]{:S(2)}) copy-start(bf16[2,256,512]{2,1,0:T(8,128)(2,1)} %constant.26.clone.back_ref) | copy-start | bytes 1572868
  4.9 43.1 %copy-start.2 = (bf16[512,512]{1,0:T(8,128)(2,1)S(1)}, bf16[512,512]{1,0:T(8,128)(2,1)}, u32[]{:S(2)}) copy-start(bf16[512,512]{1,0:T(8,128)(2,1)} %constant.25.clone.columns_ref) | copy-start | bytes 1572868
  5.0 43.1 %copy-start.4 = (bf16[256,256]{1,0:T(8,128)(2,1)S(1)}, bf16[256,256]{1,0:T(8,128)(2,1)}, u32[]{:S(2)}) copy-start(bf16[256,256]{1,0:T(8,128)(2,1)} %constant.27.clone.gather_ref) | copy-start | bytes 393220
  5.0 43.0 %all-to-all-start = ((bf16[128,33,2,128]{3,2,1,0:T(2,128)(2,1)}), bf16[128,33,2,128]{3,2,1,0:T(2,128)(2,1)S(1)}, u32[]{:S(2)}, u32[]{:S(2)}) async-start(bf16[128,33,2,128]{3,2,1,0:T(2,128)(2,1)} %forward_rows.1), calls=%async_computation | async-start | bytes 4325376 | tf_op jit(solution)/shard_map/all_to_all | solution.py:377
  53.3 35.0 %copy-start = (bf16[512,512]{1,0:T(8,128)(2,1)S(1)}, bf16[512,512]{1,0:T(8,128)(2,1)}, u32[]{:S(2)}) copy-start(bf16[512,512]{1,0:T(8,128)(2,1)} %constant.24.clone.table_ref) | copy-start | bytes 1572868
  53.3 35.0 %copy-start.3 = (bf16[256,256]{1,0:T(8,128)(2,1)S(1)}, bf16[256,256]{1,0:T(8,128)(2,1)}, u32[]{:S(2)}) copy-start(bf16[256,256]{1,0:T(8,128)(2,1)} %constant.28.clone.gather_ref) | copy-start | bytes 393220
  53.3 35.0 %all-to-all-start.1 = ((bf16[128,64,128]{2,1,0:T(8,128)(2,1)}), bf16[128,64,128]{2,1,0:T(8,128)(2,1)S(1)}, u32[]{:S(2)}, u32[]{:S(2)}) async-start(bf16[128,64,128]{2,1,0:T(8,128)(2,1)} %cross_columns.1), calls=%async_computation.1 | async-start | bytes 4194304 | tf_op jit(solution)/shard_map/all_to_all | solution.py:394

commit v4 on v3

--- a/solution.py
+++ b/solution.py
@@ -4,9 +4,12 @@
 from jax import lax
 from jax.experimental import pallas as pl
 from jax.experimental.pallas import tpu as pltpu
+from jax.sharding import Mesh
 from jax.sharding import PartitionSpec as P
 
-AXES = ("scene", "grp")
+AXES = ("x", "y", "core", "z")
+SIZES = (4, 4, 2, 4)
+ORDER = ("core", "z", "y", "x")
 LENGTH = 512
 HALF = LENGTH // 2
 SLOTS_HELD = 4
@@ -84,6 +87,11 @@
     off = local - mean
     spread = total(second - first * first * (1.0 / steps) + off * off * float(steps))
     return mean, lax.rsqrt(spread * (1.0 / entries) + 1e-05)
+
+
+def exchange_place(scene):
+    z, core, y, x = scene & 3, (scene >> 2) & 1, (scene >> 3) & 3, scene >> 5
+    return ((core * 4 + z) * 4 + y) * 4 + x
 
 
 def forward_kernel(
@@ -130,7 +138,8 @@
             column = lax.broadcasted_iota(jnp.int32, (2, LANES), 1) // (LANES // 4)
             named = jnp.zeros((2, LANES), F32)
             for k in range(4):
-                named = jnp.where(column == k, pair_ref[0, k].astype(F32), named)
+                value = pair_ref[0, k] if k % 2 else exchange_place(pair_ref[0, k])
+                named = jnp.where(column == k, value.astype(F32), named)
             names_ref[...] = jnp.broadcast_to(named[None], (devices, 2, LANES)).astype(BF16)
             write = pltpu.make_async_copy(names_ref, out_hbm.at[:, TILES - 1], late_sem.at[2])
             write.start()
@@ -347,7 +356,7 @@
 
 def per_device(windows, counts, intersection_pairs):
     devices = lax.axis_size(AXES)
-    position = lax.axis_index(AXES).astype(jnp.int32).reshape(1)
+    position = lax.axis_index(ORDER).astype(jnp.int32).reshape(1)
     forward, backward, columns, columns_back, gather_slots, gather = packed_tables(devices)
     smem = pl.BlockSpec(memory_space=pltpu.SMEM)
     vmem = pl.BlockSpec(memory_space=pltpu.VMEM)
@@ -374,7 +383,7 @@
         compiler_params=params,
         name="forward_rows",
     )(in_hbm(intersection_pairs), in_hbm(windows[0]), in_hbm(forward))
-    moved = lax.all_to_all(sent, AXES, 0, 0, tiled=True)
+    moved = lax.all_to_all(sent, ORDER, 0, 0, tiled=True)
     crossed = pl.pallas_call(
         cross_kernel,
         in_specs=[smem, vmem, vmem, vmem, vmem],
@@ -391,7 +400,7 @@
         compiler_params=params,
         name="cross_columns",
     )(position, moved, columns, columns_back, gather_slots)
-    returned = lax.all_to_all(crossed, AXES, 0, 0, tiled=True)
+    returned = lax.all_to_all(crossed, ORDER, 0, 0, tiled=True)
     return pl.pallas_call(
         surface_kernel,
         in_specs=[smem, vmem, vmem, vmem],
@@ -410,6 +419,7 @@
 def solution(mesh):
     in_specs = (P(AXES, None, None, None), P(AXES), P(AXES, None))
     out_specs = P(AXES, None, None, None)
+    split = Mesh(mesh.devices.reshape(SIZES), AXES)
     return jax.shard_map(
-        per_device, mesh=mesh, in_specs=in_specs, out_specs=out_specs, check_vma=False
-    )
+        per_device, mesh=split, in_specs=in_specs, out_specs=out_specs, check_vma=False
+    )

time: 91.5 us -> 89 us (0.973)
  waiting for transfers between devices: 61.8 us -> 57.2 us
  starting transfers between devices: 15.5 us -> 17.7 us
    all_to_all x2, waiting for transfers between devices: 61.8 us -> 57.2 us  [the longest x1 29.3 us: per_device(): moved = lax.all_to_all(sent, ORDER, 0, 0, tiled=True)]
    all_to_all x2, starting transfers between devices: 15.5 us -> 17.7 us  [the longest x1 11.5 us: per_device(): moved = lax.all_to_all(sent, ORDER, 0, 0, tiled=True)]
where the time goes in v4:
time: 89 us; the launch traced here: 88.8 us
  waiting for transfers between devices  57.2 us (64%)
  starting transfers between devices  17.7 us (20%)
  Pallas kernels  13.1 us (15%)
    all_to_all x1, waiting for transfers between devices, per_device(): moved = lax.all_to_all(sent, ORDER, 0, 0, tiled=True)  29.3 us
    all_to_all x1, waiting for transfers between devices, per_device(): returned = lax.all_to_all(crossed, ORDER, 0, 0, tiled=True)  28 us
    all_to_all x1, starting transfers between devices, per_device(): moved = lax.all_to_all(sent, ORDER, 0, 0, tiled=True)  11.5 us
    all_to_all x1, starting transfers between devices, per_device(): returned = lax.all_to_all(crossed, ORDER, 0, 0, tiled=True)  6.17 us
    pallas_call x1, Pallas kernels, per_device(): pl.pallas_call(cross_kernel, in_specs=[smem, vmem, vmem, vmem, vmem], out...  5.28 us
    pallas_call x1, Pallas kernels, per_device(): pl.pallas_call(forward_kernel, in_specs=[hbm, hbm, hbm], out_specs=hbm, o...  4.93 us
    pallas_call x1, Pallas kernels, per_device(): pl.pallas_call(surface_kernel, in_specs=[smem, vmem, vmem, vmem], out_spe...  2.92 us
  transfers between devices with their start and end apart: 2, of which 2 were waited for; matrix products, arithmetic and copies ran while one was open for 0% of the time, Pallas kernels for 0%

profile of v4, /device:TPU:1, one launch (start us, length us, event | category | flops | bytes accessed | tf_op | source)
XLA Modules:
  0.0 88.8 jit_solution(4327818095279773744)
XLA Ops:
  0.0 4.9 %forward_rows.1 = bf16[128,33,2,128]{3,2,1,0:T(2,128)(2,1)} custom-call(s32[1,4]{1,0:T(1,128)} %pair_hbm.1, bf16[4,512,512]{2,1,0:T(8,128)(2,1)} %bitcast.2, bf16[512,512]{1,0:T(8,128)(2,1)} %constant.34.clone.table_hbm), custom_call_target="tpu_custom_call" | custom-call | tf_op jit(solution)/shard_map/forward_rows/pallas_call | solution.py:368
  4.9 0.0 copy-start.1
  4.9 0.0 copy-start.2
  5.0 0.0 copy-start.4
  5.0 11.5 %all-to-all-start = ((bf16[128,33,2,128]{3,2,1,0:T(2,128)(2,1)}), bf16[128,33,2,128]{3,2,1,0:T(2,128)(2,1)S(1)}, u32[]{:S(2)}, u32[]{:S(2)}) async-start(bf16[128,33,2,128]{3,2,1,0:T(2,128)(2,1)} %forward_rows.1), calls=%async_computation | async-start | bytes 4325376 | tf_op jit(solution)/shard_map/all_to_all | solution.py:386
  16.5 29.3 %all-to-all-done.m_ref = bf16[128,33,2,128]{3,2,1,0:T(2,128)(2,1)S(1)} async-done(((bf16[128,33,2,128]{3,2,1,0:T(2,128)(2,1)}), bf16[128,33,2,128]{3,2,1,0:T(2,128)(2,1)S(1)}, u32[]{:S(2)}, u32[]{:S(2)}) %all-to-all-start) | async-done | bytes 2162720 | tf_op jit(solution)/shard_map/all_to_all | solution.py:386
  45.7 0.0 copy-done.1
  45.8 0.0 copy-done.2
  45.8 0.0 copy-done.4
  45.8 5.3 %cross_columns.1 = bf16[128,64,128]{2,1,0:T(8,128)(2,1)} custom-call(s32[1]{0:T(128)} %bitcast.first_ref, bf16[128,33,2,128]{3,2,1,0:T(2,128)(2,1)S(1)} %all-to-all-done.m_ref, bf16[512,512]{1,0:T(8,128)(2,1)S(1)} %copy-done.2, bf16[2,256,512]{2,1,0:T(8,128)(2,1)S(1)} %copy-done.1, bf16[256,256]{1,0:T(8,128)(2,1)S(1)} %copy-done.4), custom_call_target="tpu_custom_call" | custom-call | tf_op jit(solution)/shard_map/cross_columns/pallas_call | solution.py:387
  51.1 0.0 copy-start
  51.1 0.0 copy-start.3
  51.1 6.2 %all-to-all-start.1 = ((bf16[128,64,128]{2,1,0:T(8,128)(2,1)}), bf16[128,64,128]{2,1,0:T(8,128)(2,1)S(1)}, u32[]{:S(2)}, u32[]{:S(2)}) async-start(bf16[128,64,128]{2,1,0:T(8,128)(2,1)} %cross_columns.1), calls=%async_computation.1 | async-start | bytes 4194304 | tf_op jit(solution)/shard_map/all_to_all | solution.py:403
  57.9 28.0 %all-to-all-done.1.m_ref = bf16[128,64,128]{2,1,0:T(8,128)(2,1)S(1)} async-done(((bf16[128,64,128]{2,1,0:T(8,128)(2,1)}), bf16[128,64,128]{2,1,0:T(8,128)(2,1)S(1)}, u32[]{:S(2)}, u32[]{:S(2)}) %all-to-all-start.1) | async-done | bytes 2097184 | tf_op jit(solution)/shard_map/all_to_all | solution.py:403
  85.9 0.0 copy-done
  85.9 0.0 copy-done.3
  85.9 2.9 %surfaces.1 = f32[1,4,512,512]{3,2,1,0:T(8,128)} custom-call(s32[1]{0:T(128)S(6)} %copy.10.count_ref, bf16[128,64,128]{2,1,0:T(8,128)(2,1)S(1)} %all-to-all-done.1.m_ref, bf16[512,512]{1,0:T(8,128)(2,1)S(1)} %copy-done, bf16[256,256]{1,0:T(8,128)(2,1)S(1)} %copy-done.3), custom_call_target="tpu_custom_call" | custom-call | tf_op jit(solution)/shard_map/surfaces/pallas_call | solution.py:404
Async XLA Ops:
  4.9 40.8 %copy-start.1 = (bf16[2,256,512]{2,1,0:T(8,128)(2,1)S(1)}, bf16[2,256,512]{2,1,0:T(8,128)(2,1)}, u32[]{:S(2)}) copy-start(bf16[2,256,512]{2,1,0:T(8,128)(2,1)} %constant.37.clone.back_ref) | copy-start | bytes 1572868
  4.9 40.8 %copy-start.2 = (bf16[512,512]{1,0:T(8,128)(2,1)S(1)}, bf16[512,512]{1,0:T(8,128)(2,1)}, u32[]{:S(2)}) copy-start(bf16[512,512]{1,0:T(8,128)(2,1)} %constant.36.clone.columns_ref) | copy-start | bytes 1572868
  5.0 40.8 %copy-start.4 = (bf16[256,256]{1,0:T(8,128)(2,1)S(1)}, bf16[256,256]{1,0:T(8,128)(2,1)}, u32[]{:S(2)}) copy-start(bf16[256,256]{1,0:T(8,128)(2,1)} %constant.38.clone.gather_ref) | copy-start | bytes 393220
  5.0 40.8 %all-to-all-start = ((bf16[128,33,2,128]{3,2,1,0:T(2,128)(2,1)}), bf16[128,33,2,128]{3,2,1,0:T(2,128)(2,1)S(1)}, u32[]{:S(2)}, u32[]{:S(2)}) async-start(bf16[128,33,2,128]{3,2,1,0:T(2,128)(2,1)} %forward_rows.1), calls=%async_computation | async-start | bytes 4325376 | tf_op jit(solution)/shard_map/all_to_all | solution.py:386
  51.1 34.8 %copy-start = (bf16[512,512]{1,0:T(8,128)(2,1)S(1)}, bf16[512,512]{1,0:T(8,128)(2,1)}, u32[]{:S(2)}) copy-start(bf16[512,512]{1,0:T(8,128)(2,1)} %constant.35.clone.table_ref) | copy-start | bytes 1572868
  51.1 34.8 %copy-start.3 = (bf16[256,256]{1,0:T(8,128)(2,1)S(1)}, bf16[256,256]{1,0:T(8,128)(2,1)}, u32[]{:S(2)}) copy-start(bf16[256,256]{1,0:T(8,128)(2,1)} %constant.39.clone.gather_ref) | copy-start | bytes 393220
  51.1 34.8 %all-to-all-start.1 = ((bf16[128,64,128]{2,1,0:T(8,128)(2,1)}), bf16[128,64,128]{2,1,0:T(8,128)(2,1)S(1)}, u32[]{:S(2)}, u32[]{:S(2)}) async-start(bf16[128,64,128]{2,1,0:T(8,128)(2,1)} %cross_columns.1), calls=%async_computation.1 | async-start | bytes 4194304 | tf_op jit(solution)/shard_map/all_to_all | solution.py:403

commit v5 on v4

--- a/solution.py
+++ b/solution.py
@@ -124,15 +124,17 @@
     spectra = []
     writes = []
     for s in range(SLOTS_HELD):
-        reads[s].wait()
-        mean, scale = moments(x_ref, s)
-        if s == 0:
+        if s % 2 == 0:
+            continue
+        for t in (s - 1, s):
+            reads[t].wait()
+        if s == 1:
             table_read.wait()
             row_sum = jnp.dot(table_ref[...], ones, preferred_element_type=F32)
-        product = jnp.dot(table_ref[...], x_ref[s], preferred_element_type=F32)
-        spectra.append(split_rows(product * scale - wide(row_sum * (mean * scale)), 8))
-        if s % 2 == 0:
-            continue
+        for t in (s - 1, s):
+            mean, scale = moments(x_ref, t)
+            product = jnp.dot(table_ref[...], x_ref[t], preferred_element_type=F32)
+            spectra.append(split_rows(product * scale - wide(row_sum * (mean * scale)), 8))
         if s == 1:
             pair_read.wait()
             column = lax.broadcasted_iota(jnp.int32, (2, LANES), 1) // (LANES // 4)
@@ -176,12 +178,7 @@
 
 
 def rows_of_8(rows_ref, block):
-    tile = lambda k: (
-        rows_ref[block * 16 : (block + 1) * 16, k * 8 : (k + 1) * 8]
-        .astype(F32)
-        .reshape(128, LANES)
-        .astype(BF16)
-    )
+    tile = lambda k: rows_ref[block * 16 : (block + 1) * 16, k * 8 : (k + 1) * 8].reshape(128, LANES)
     return jnp.concatenate(
         [
             jnp.concatenate([tile(lane), tile(LANE_BLOCKS + lane)], axis=0)

time: 89 us -> 88.9 us (level)
  no operation moved by 1% of the time
where the time goes in v5:
time: 88.9 us; the launch traced here: 88.7 us
  waiting for transfers between devices  57.2 us (64%)
  starting transfers between devices  17.7 us (20%)
  Pallas kernels  13.1 us (15%)
    all_to_all x1, waiting for transfers between devices, per_device(): moved = lax.all_to_all(sent, ORDER, 0, 0, tiled=True)  29.3 us
    all_to_all x1, waiting for transfers between devices, per_device(): returned = lax.all_to_all(crossed, ORDER, 0, 0, tiled=True)  28 us
    all_to_all x1, starting transfers between devices, per_device(): moved = lax.all_to_all(sent, ORDER, 0, 0, tiled=True)  11.5 us
    all_to_all x1, starting transfers between devices, per_device(): returned = lax.all_to_all(crossed, ORDER, 0, 0, tiled=True)  6.16 us
    pallas_call x1, Pallas kernels, per_device(): pl.pallas_call(cross_kernel, in_specs=[smem, vmem, vmem, vmem, vmem], out...  5.29 us
    pallas_call x1, Pallas kernels, per_device(): pl.pallas_call(forward_kernel, in_specs=[hbm, hbm, hbm], out_specs=hbm, o...  4.85 us
    pallas_call x1, Pallas kernels, per_device(): pl.pallas_call(surface_kernel, in_specs=[smem, vmem, vmem, vmem], out_spe...  2.92 us
  transfers between devices with their start and end apart: 2, of which 2 were waited for; matrix products, arithmetic and copies ran while one was open for 0% of the time, Pallas kernels for 0%

profile of v5, /device:TPU:1, one launch (start us, length us, event | category | flops | bytes accessed | tf_op | source)
XLA Modules:
  0.0 88.7 jit_solution(3012676225068179803)
XLA Ops:
  0.0 4.8 %forward_rows.1 = bf16[128,33,2,128]{3,2,1,0:T(2,128)(2,1)} custom-call(s32[1,4]{1,0:T(1,128)} %pair_hbm.1, bf16[4,512,512]{2,1,0:T(8,128)(2,1)} %bitcast.2, bf16[512,512]{1,0:T(8,128)(2,1)} %constant.34.clone.table_hbm), custom_call_target="tpu_custom_call" | custom-call | tf_op jit(solution)/shard_map/forward_rows/pallas_call | solution.py:365
  4.9 0.0 copy-start.1
  4.9 0.0 copy-start.2
  4.9 0.0 copy-start.4
  4.9 11.5 %all-to-all-start = ((bf16[128,33,2,128]{3,2,1,0:T(2,128)(2,1)}), bf16[128,33,2,128]{3,2,1,0:T(2,128)(2,1)S(1)}, u32[]{:S(2)}, u32[]{:S(2)}) async-start(bf16[128,33,2,128]{3,2,1,0:T(2,128)(2,1)} %forward_rows.1), calls=%async_computation | async-start | bytes 4325376 | tf_op jit(solution)/shard_map/all_to_all | solution.py:383
  16.4 29.3 %all-to-all-done.m_ref = bf16[128,33,2,128]{3,2,1,0:T(2,128)(2,1)S(1)} async-done(((bf16[128,33,2,128]{3,2,1,0:T(2,128)(2,1)}), bf16[128,33,2,128]{3,2,1,0:T(2,128)(2,1)S(1)}, u32[]{:S(2)}, u32[]{:S(2)}) %all-to-all-start) | async-done | bytes 2162720 | tf_op jit(solution)/shard_map/all_to_all | solution.py:383
  45.7 0.0 copy-done.1
  45.7 0.0 copy-done.2
  45.7 0.0 copy-done.4
  45.7 5.3 %cross_columns.1 = bf16[128,64,128]{2,1,0:T(8,128)(2,1)} custom-call(s32[1]{0:T(128)} %bitcast.first_ref, bf16[128,33,2,128]{3,2,1,0:T(2,128)(2,1)S(1)} %all-to-all-done.m_ref, bf16[512,512]{1,0:T(8,128)(2,1)S(1)} %copy-done.2, bf16[2,256,512]{2,1,0:T(8,128)(2,1)S(1)} %copy-done.1, bf16[256,256]{1,0:T(8,128)(2,1)S(1)} %copy-done.4), custom_call_target="tpu_custom_call" | custom-call | tf_op jit(solution)/shard_map/cross_columns/pallas_call | solution.py:384
  51.0 0.0 copy-start
  51.0 0.0 copy-start.3
  51.0 6.2 %all-to-all-start.1 = ((bf16[128,64,128]{2,1,0:T(8,128)(2,1)}), bf16[128,64,128]{2,1,0:T(8,128)(2,1)S(1)}, u32[]{:S(2)}, u32[]{:S(2)}) async-start(bf16[128,64,128]{2,1,0:T(8,128)(2,1)} %cross_columns.1), calls=%async_computation.1 | async-start | bytes 4194304 | tf_op jit(solution)/shard_map/all_to_all | solution.py:400
  57.8 28.0 %all-to-all-done.1.m_ref = bf16[128,64,128]{2,1,0:T(8,128)(2,1)S(1)} async-done(((bf16[128,64,128]{2,1,0:T(8,128)(2,1)}), bf16[128,64,128]{2,1,0:T(8,128)(2,1)S(1)}, u32[]{:S(2)}, u32[]{:S(2)}) %all-to-all-start.1) | async-done | bytes 2097184 | tf_op jit(solution)/shard_map/all_to_all | solution.py:400
  85.8 0.0 copy-done
  85.8 0.0 copy-done.3
  85.8 2.9 %surfaces.1 = f32[1,4,512,512]{3,2,1,0:T(8,128)} custom-call(s32[1]{0:T(128)S(6)} %copy.10.count_ref, bf16[128,64,128]{2,1,0:T(8,128)(2,1)S(1)} %all-to-all-done.1.m_ref, bf16[512,512]{1,0:T(8,128)(2,1)S(1)} %copy-done, bf16[256,256]{1,0:T(8,128)(2,1)S(1)} %copy-done.3), custom_call_target="tpu_custom_call" | custom-call | tf_op jit(solution)/shard_map/surfaces/pallas_call | solution.py:401
Async XLA Ops:
  4.9 40.8 %copy-start.1 = (bf16[2,256,512]{2,1,0:T(8,128)(2,1)S(1)}, bf16[2,256,512]{2,1,0:T(8,128)(2,1)}, u32[]{:S(2)}) copy-start(bf16[2,256,512]{2,1,0:T(8,128)(2,1)} %constant.37.clone.back_ref) | copy-start | bytes 1572868
  4.9 40.8 %copy-start.2 = (bf16[512,512]{1,0:T(8,128)(2,1)S(1)}, bf16[512,512]{1,0:T(8,128)(2,1)}, u32[]{:S(2)}) copy-start(bf16[512,512]{1,0:T(8,128)(2,1)} %constant.36.clone.columns_ref) | copy-start | bytes 1572868
  4.9 40.8 %copy-start.4 = (bf16[256,256]{1,0:T(8,128)(2,1)S(1)}, bf16[256,256]{1,0:T(8,128)(2,1)}, u32[]{:S(2)}) copy-start(bf16[256,256]{1,0:T(8,128)(2,1)} %constant.38.clone.gather_ref) | copy-start | bytes 393220
  4.9 40.8 %all-to-all-start = ((bf16[128,33,2,128]{3,2,1,0:T(2,128)(2,1)}), bf16[128,33,2,128]{3,2,1,0:T(2,128)(2,1)S(1)}, u32[]{:S(2)}, u32[]{:S(2)}) async-start(bf16[128,33,2,128]{3,2,1,0:T(2,128)(2,1)} %forward_rows.1), calls=%async_computation | async-start | bytes 4325376 | tf_op jit(solution)/shard_map/all_to_all | solution.py:383
  51.0 34.8 %copy-start = (bf16[512,512]{1,0:T(8,128)(2,1)S(1)}, bf16[512,512]{1,0:T(8,128)(2,1)}, u32[]{:S(2)}) copy-start(bf16[512,512]{1,0:T(8,128)(2,1)} %constant.35.clone.table_ref) | copy-start | bytes 1572868
  51.0 34.8 %copy-start.3 = (bf16[256,256]{1,0:T(8,128)(2,1)S(1)}, bf16[256,256]{1,0:T(8,128)(2,1)}, u32[]{:S(2)}) copy-start(bf16[256,256]{1,0:T(8,128)(2,1)} %constant.39.clone.gather_ref) | copy-start | bytes 393220
  51.0 34.8 %all-to-all-start.1 = ((bf16[128,64,128]{2,1,0:T(8,128)(2,1)}), bf16[128,64,128]{2,1,0:T(8,128)(2,1)S(1)}, u32[]{:S(2)}, u32[]{:S(2)}) async-start(bf16[128,64,128]{2,1,0:T(8,128)(2,1)} %cross_columns.1), calls=%async_computation.1 | async-start | bytes 4194304 | tf_op jit(solution)/shard_map/all_to_all | solution.py:400
